TPU v7x, 32 devices: a whole 2x2x4 slice. The times are simulated.
32 devices in a mesh: grp: 8 (over y, x, core), tp: 4 (over z).
Axes of the slice: x: 2, y: 2, z: 4, core: 2. Of those that a mesh axis runs over, the one named last changes fastest.
Arguments:
- sel_hidden: bfloat16 [16, 320, 4096], P('grp'), may hold values from -6 to 6
- norm_gain: float32 [4096], replicated, may hold values from 0.25 to 1.75
- w_query: bfloat16 [4096, 4096], P(None, 'tp'), may hold values from -0.09375 to 0.09375
- w_key: bfloat16 [4096, 1024], P(None, 'tp'), may hold values from -0.1875 to 0.1875
- w_value: bfloat16 [4096, 1024], P(None, 'tp'), may hold values from -0.09375 to 0.09375
- w_out: bfloat16 [4096, 4096], P(None, 'tp'), may hold values from -0.09375 to 0.09375
- doc_cache: bfloat16 [128, 2, 512, 1024], P('grp', None, None, 'tp'), may hold values from -250 to 250
- home: int32 [128], replicated, may hold values from 0 to 127, as said below
- doc_ids: int32 [16, 8], replicated, may hold values from 0 to 127, as said below
- doc_len: int32 [128], replicated, may hold values from 128 to 512, as said below
- positions: int32 [16, 320], P('grp'), may hold values from 0 to 4095, as said below
Outputs:
- mixed: bfloat16 [16, 320, 4096], P('grp', None, 'tp')
Inputs may be any that keep to these rules, and one draw needn't show every extreme that they name: `home`: a permutation: every location holds one document; the owner of location l along grp is l // 16. `doc_ids`: requests g * 2 .. (g + 1) * 2 - 1 form serving group g; the 16 documents of one group all differ, no owner holds more than 2 of them, and in every group at least one owner holds exactly 2. `doc_len`: documents doc_ids[0, 0] and doc_ids[0, 7] have length 512 (others may too). positions: each row rises; for each j it holds 40 positions j * 512 + t with t below the length of document doc_ids[r, j].
All inputs are finite; a program needn't handle non-finite values.
Results may differ from a plain program's by a relative error of at most 0.006.
The roundings to bfloat16 on the way count: a program that leaves them out, or rounds other values in their place, can miss the bound.
Values may be sent and summed in bfloat16 or wider, within the bound.
A program may use at most 192 MiB of HBM per device.

v0:
```python
import functools

import jax
import jax.numpy as jnp
from jax import lax
from jax.experimental import pallas as pl
from jax.experimental.pallas import tpu as pltpu
from jax.sharding import PartitionSpec as P

H = 32
KVH = 8
HD = 128
CAP = 2
PAIR = 2
LANES = 128
MASKED = -1e30
LOG2E = 1.4426950408889634


def attention_kernel(retrieved, doc_rows, tokens, slots, lens, *refs):
    docs = refs[:retrieved]
    q_ref, new_k, new_v, pos_lane, pos_col, o_ref = refs[retrieved : retrieved + 6]
    keys, values, scores, top, total, acc = refs[retrieved + 6 :]
    group = H // KVH
    picks = tokens // retrieved
    span = PAIR * picks
    factor = HD ** (-0.5) * LOG2E
    request = pl.program_id(0)
    block = pl.program_id(1)

    @pl.when(block == 0)
    def blend():
        for j in range(retrieved):
            low = j * picks // LANES * LANES
            high = min(tokens, -(-(j + 1) * picks // LANES) * LANES)
            at = lax.broadcasted_iota(jnp.int32, (doc_rows, high - low), 0) + j * doc_rows
            hit = jnp.where(at == pos_lane[0, :, low:high], 1.0, 0.0).astype(jnp.bfloat16)
            ones = jnp.ones((high - low, HD), jnp.bfloat16)
            fresh = jnp.concatenate([new_k[low:high, :], new_v[low:high, :], ones], axis=1)
            placed = jnp.dot(hit, fresh, preferred_element_type=jnp.float32)
            replaced = placed[:, 2 * HD :] > 0.5
            keys[j] = jnp.where(
                replaced, placed[:, :HD], docs[j][0, 0].astype(jnp.float32)
            ).astype(jnp.bfloat16)
            values[j] = jnp.where(
                replaced, placed[:, HD : 2 * HD], docs[j][0, 1].astype(jnp.float32)
            ).astype(jnp.bfloat16)

    query = jnp.concatenate([q_ref[:, g * HD : (g + 1) * HD] for g in range(group)], axis=0)
    top[...] = jnp.full_like(top, MASKED)
    total[...] = jnp.zeros_like(total)
    acc[...] = jnp.zeros_like(acc)

    def score(j, mask_of):
        raw = lax.dot_general(
            query, keys[j], (((1,), (1,)), ((), ())), preferred_element_type=jnp.float32
        )
        mask = mask_of(j)
        for g in range(group):
            rows = slice(g * span, (g + 1) * span)
            part = jnp.where(mask, raw[rows, :], MASKED)
            scores[j, rows, :] = part
            best = top[rows, :]
            for n in range(doc_rows // LANES):
                best = jnp.maximum(best, part[:, n * LANES : (n + 1) * LANES])
            top[rows, :] = best

    def mask_full(j):
        length = lens[request * retrieved + j]
        return lax.broadcasted_iota(jnp.int32, (1, doc_rows), 1) < length

    def mask_diagonal(j):
        length = lens[request * retrieved + j]
        limit = jnp.minimum(pos_col[...] - j * doc_rows, length - 1)
        return lax.broadcasted_iota(jnp.int32, (span, doc_rows), 1) <= limit

    first = block * PAIR
    last = first + PAIR

    @pl.loop(0, first)
    def _(j):
        score(j, mask_full)

    for n in range(PAIR):
        score(first + n, mask_diagonal)

    peak = jnp.max(top[...], axis=1, keepdims=True) * factor
    top[...] = jnp.broadcast_to(peak, top.shape)

    @pl.loop(0, last)
    def _(j):
        for g in range(group):
            rows = slice(g * span, (g + 1) * span)
            shift = top[rows, :]
            add = total[rows, :]
            for n in range(doc_rows // LANES):
                cols = slice(n * LANES, (n + 1) * LANES)
                expo = jnp.exp2(scores[j, rows, cols] * factor - shift)
                scores[j, rows, cols] = expo
                add = add + expo
            total[rows, :] = add

    inverse = 1.0 / jnp.sum(total[...], axis=1, keepdims=True)
    total[...] = jnp.broadcast_to(inverse, total.shape)

    @pl.loop(0, last)
    def _(j):
        scale = total[...]
        weights = jnp.concatenate(
            [
                (scores[j, :, n * LANES : (n + 1) * LANES] * scale).astype(jnp.bfloat16)
                for n in range(doc_rows // LANES)
            ],
            axis=1,
        )
        acc[...] += jnp.dot(weights, values[j], preferred_element_type=jnp.float32)

    for g in range(group):
        o_ref[:, g * HD : (g + 1) * HD] = acc[g * span : (g + 1) * span, :].astype(o_ref.dtype)


def attention(head, cache, slots, lens, query, key_new, value_new, positions):
    served, tokens = positions.shape
    retrieved = slots.shape[0] // served
    doc_rows = cache.shape[2]
    group = H // KVH
    span = tokens // retrieved * PAIR
    blocks = retrieved // PAIR
    rows = group * span
    doc_specs = [
        pl.BlockSpec(
            (1, 2, doc_rows, HD),
            lambda r, b, slots, lens, j=j: (slots[r * retrieved + j], 0, 0, 0),
        )
        for j in range(retrieved)
    ]
    pairs = served * tokens * group * retrieved * doc_rows * 5 // 8
    return pl.pallas_call(
        functools.partial(attention_kernel, retrieved, doc_rows, tokens),
        grid_spec=pltpu.PrefetchScalarGridSpec(
            num_scalar_prefetch=2,
            grid=(served, blocks),
            in_specs=doc_specs
            + [
                pl.BlockSpec((span, group * HD), lambda r, b, *_: (r * blocks + b, head)),
                pl.BlockSpec((tokens, HD), lambda r, b, *_: (r, head)),
                pl.BlockSpec((tokens, HD), lambda r, b, *_: (r, head)),
                pl.BlockSpec((1, 1, tokens), lambda r, b, *_: (r, 0, 0)),
                pl.BlockSpec((span, 1), lambda r, b, *_: (r * blocks + b, 0)),
            ],
            out_specs=pl.BlockSpec((span, group * HD), lambda r, b, *_: (r * blocks + b, 0)),
            scratch_shapes=[
                pltpu.VMEM((retrieved, doc_rows, HD), jnp.bfloat16),
                pltpu.VMEM((retrieved, doc_rows, HD), jnp.bfloat16),
                pltpu.VMEM((retrieved, rows, doc_rows), jnp.float32),
                pltpu.VMEM((rows, LANES), jnp.float32),
                pltpu.VMEM((rows, LANES), jnp.float32),
                pltpu.VMEM((rows, HD), jnp.float32),
            ],
        ),
        out_shape=jax.ShapeDtypeStruct((served * tokens, group * HD), jnp.bfloat16),
        compiler_params=pltpu.CompilerParams(vmem_limit_bytes=40 * 2**20),
        cost_estimate=pl.CostEstimate(
            flops=8 * pairs * HD,
            bytes_accessed=2 * served * retrieved * doc_rows * 2 * HD,
            transcendentals=pairs,
        ),
    )(
        slots,
        lens,
        *([cache] * retrieved),
        query,
        key_new,
        value_new,
        positions[:, None, :],
        positions.reshape(served * tokens, 1),
    )


def body(
    sel_hidden,
    norm_gain,
    w_query,
    w_key,
    w_value,
    w_out,
    doc_cache,
    home,
    doc_ids,
    doc_len,
    positions,
):
    groups = lax.axis_size("grp")
    me = lax.axis_index("grp")
    stored = doc_cache.shape[0]
    doc_rows = doc_cache.shape[2]
    width = doc_cache.shape[3]
    kv_local = width // HD
    group = H // KVH
    served = sel_hidden.shape[0]
    tokens = sel_hidden.shape[1]
    retrieved = doc_ids.shape[1]
    per_group = served * retrieved
    location = home[doc_ids].reshape(groups, per_group)
    owner = location // stored
    slot_index = location % stored
    slots = jnp.arange(per_group, dtype=jnp.int32)
    earlier = (owner[:, :, None] == owner[:, None, :]) & (
        slots[None, None, :] < slots[None, :, None]
    )
    rank = jnp.sum(earlier.astype(jnp.int32), axis=2)
    match = (owner == me)[:, :, None] & (
        rank[:, :, None] == jnp.arange(CAP, dtype=jnp.int32)[None, None, :]
    )
    chosen = jnp.sum(jnp.where(match, slot_index[:, :, None], 0), axis=1)
    own_slots = owner[me] * CAP + rank[me]
    lengths = doc_len[doc_ids.reshape(groups, per_group)[me]]

    incoming = []
    for head in range(kv_local):
        outgoing = doc_cache[:, :, :, head * HD : (head + 1) * HD][chosen]
        if incoming:
            outgoing, incoming[-1] = lax.optimization_barrier((outgoing, incoming[-1]))
        incoming.append(
            lax.all_to_all(outgoing, "grp", split_axis=0, concat_axis=0, tiled=True)
        )

    xf = sel_hidden.astype(jnp.float32)
    normed = (xf * lax.rsqrt(jnp.mean(xf * xf, axis=-1, keepdims=True) + 1e-05) * norm_gain).astype(
        jnp.bfloat16
    )
    normed_rows = normed.reshape(served * tokens, normed.shape[2])
    query = jnp.dot(normed_rows, w_query, preferred_element_type=jnp.float32).astype(jnp.bfloat16)
    key_new = jnp.dot(normed_rows, w_key, preferred_element_type=jnp.float32).astype(jnp.bfloat16)
    value_new = jnp.dot(normed_rows, w_value, preferred_element_type=jnp.float32).astype(
        jnp.bfloat16
    )

    w_heads = w_out.reshape(-1, kv_local, group * HD, w_out.shape[1])
    mixed = 0.0
    for head in range(kv_local):
        cache = incoming[head].reshape((groups * CAP, 2, doc_rows, HD))
        attn = attention(
            head, cache, own_slots, lengths, query, key_new, value_new, positions
        )
        gathered = lax.all_gather(attn, "tp", axis=1, tiled=True)
        part = w_heads[:, head].reshape(-1, w_out.shape[1])
        mixed = mixed + jnp.dot(gathered, part, preferred_element_type=jnp.float32)
    return mixed.astype(jnp.bfloat16).reshape(served, tokens, w_out.shape[1])


def solution(mesh):
    return jax.shard_map(
        body,
        mesh=mesh,
        in_specs=(
            P("grp", None, None),
            P(),
            P(None, "tp"),
            P(None, "tp"),
            P(None, "tp"),
            P(None, "tp"),
            P("grp", None, None, "tp"),
            P(),
            P(),
            P(),
            P("grp", None),
        ),
        out_specs=P("grp", None, "tp"),
        check_vma=False,
    )
```

profile of v0, /device:TPU:0, one launch (start us, length us, event | category | flops | bytes accessed | tf_op | source)
XLA Modules:
  0.0 238.2 jit_solution(16026315822615711633)
XLA Ops:
  6.5 0.0 copy-start
  6.5 0.0 copy-start.2
  6.6 0.8 compare_select_fusion
  7.4 0.1 copy.20
  7.5 0.1 reshape.191
  7.6 0.0 copy-done.2
  7.6 1.2 gather_fusion
  8.8 0.1 reshape.181
  8.9 0.3 convert_reduce_fusion
  9.2 0.2 select_reduce_fusion
  9.4 0.1 copy.22
  9.5 0.1 reshape.207
  9.6 6.0 %fusion.12 = (bf16[16,2,512,128]{3,2,1,0:T(8,128)(2,1)}, bf16[16,2,512,128]{3,2,1,0:T(8,128)(2,1)}) fusion(bf16[16,2,512,256]{3,2,1,0:T(8,128)(2,1)} %param.17), kind=kLoop, calls=%fused_computation.43 | loop fusion | bytes 16777216 | tf_op jit(solution)/shard_map/slice | solution.py:221
  15.5 5.2 %gather_fusion.3 = bf16[16,2,512,128]{3,2,1,0:T(8,128)(2,1)} fusion(bf16[16,2,512,128]{3,2,1,0:T(8,128)(2,1)} %get-tuple-element.13, s32[1024]{0:T(1024)S(1)} %pad_clamp_fusion), kind=kCustom, calls=%fused_computation.3 | custom fusion | bytes 8388672 | tf_op jit(solution)/shard_map/gather | solution.py:221
  20.7 0.0 copy-start.5
  20.7 0.0 copy-start.6
  20.7 5.3 %all-to-all-start = ((bf16[8,2,2,512,128]{4,3,2,1,0:T(8,128)(2,1)}), bf16[8,2,2,512,128]{4,3,2,1,0:T(8,128)(2,1)}, u32[]{:S(2)}, u32[]{:S(2)}) async-start(bf16[8,2,2,512,128]{4,3,2,1,0:T(8,128)(2,1)} %bitcast.34), calls=%async_computation | async-start | bytes 8388608 | tf_op jit(solution)/shard_map/all_to_all | solution.py:225
  26.0 0.0 copy-done.5
  26.0 0.1 copy.21
  26.1 0.0 copy-done.6
  26.1 0.2 reshape.226.refs_12_
  26.4 5.2 %gather_fusion.2 = bf16[16,2,512,128]{3,2,1,0:T(8,128)(2,1)} fusion(bf16[16,2,512,128]{3,2,1,0:T(8,128)(2,1)} %get-tuple-element.14, s32[1024]{0:T(1024)S(1)} %pad_clamp_fusion), kind=kCustom, calls=%fused_computation.2 | custom fusion | bytes 8388672 | tf_op jit(solution)/shard_map/gather | solution.py:221
  31.6 0.0 copy-start.3
  31.6 0.0 copy-start.4
  31.6 0.1 reshape.182
  31.7 3.6 %fusion = f32[2,320]{1,0:T(2,128)S(1)} fusion(bf16[2,320,4096]{2,1,0:T(8,128)(2,1)} %param.11), kind=kLoop, calls=%fused_computation.6 | loop fusion | flops 7863680 | bytes 5245440 | tf_op jit(solution)/shard_map/reduce_sum | solution.py:229
  35.3 0.0 copy-done.3
  35.3 0.7 gather_fusion.1
  36.0 0.0 copy-done.4
  36.0 4.4 %fusion.2 = bf16[2,320,4096]{2,1,0:T(8,128)(2,1)S(1)} fusion(bf16[2,320,4096]{2,1,0:T(8,128)(2,1)} %param.11, f32[4096]{0:T(1024)S(1)} %copy-done.4, f32[2,320]{1,0:T(2,128)S(1)} %add_rsqrt_fusion), kind=kLoop, calls=%fused_computation.8 | loop fusion | flops 10485760 | bytes 10504704 | tf_op jit(solution)/shard_map/convert_element_type | solution.py:229
  40.4 0.0 copy-done
  40.4 0.0 copy-start.7
  40.4 0.0 slice-start
  40.4 1.5 convolution_convert_fusion.1.refs_10_
  42.0 0.0 copy-done.7
  42.0 0.0 slice-start.1
  42.0 1.5 convolution_convert_fusion.2.refs_9_
  43.5 0.0 slice-done
  43.5 1.1 slice-done.1
  44.7 5.6 %convolution_convert_fusion.refs_8_ = bf16[640,1024]{1,0:T(8,128)(2,1)S(1)} fusion(bf16[640,4096]{1,0:T(8,128)(2,1)S(1)} %bitcast.38, bf16[4096,1024]{1,0:T(8,128)(2,1)S(1)} %bitcast.42), kind=kOutput, calls=%fused_computation.10 | convolution fusion | flops 5369364480 | bytes 14942208 | tf_op jit(solution)/shard_map/dot_general | solution.py:233
  50.3 24.9 %all-to-all-done = bf16[8,2,2,512,128]{4,3,2,1,0:T(8,128)(2,1)} async-done(((bf16[8,2,2,512,128]{4,3,2,1,0:T(8,128)(2,1)}), bf16[8,2,2,512,128]{4,3,2,1,0:T(8,128)(2,1)}, u32[]{:S(2)}, u32[]{:S(2)}) %all-to-all-start) | async-done | bytes 4194336 | tf_op jit(solution)/shard_map/all_to_all | solution.py:225
  75.2 4.6 %all-to-all-start.1 = ((bf16[8,2,2,512,128]{4,3,2,1,0:T(8,128)(2,1)}), bf16[8,2,2,512,128]{4,3,2,1,0:T(8,128)(2,1)}, u32[]{:S(2)}, u32[]{:S(2)}) async-start(bf16[8,2,2,512,128]{4,3,2,1,0:T(8,128)(2,1)} %bitcast.33), calls=%async_computation.1 | async-start | bytes 8388608 | tf_op jit(solution)/shard_map/all_to_all | solution.py:225
  79.8 0.2 all-gather.3.cloned.1.call-start
  80.1 31.2 %shard_map.109 = bf16[640,512]{1,0:T(8,128)(2,1)} custom-call(s32[16]{0:T(128)S(1)} %fusion.10.slots, s32[16]{0:T(128)S(1)} %gather_fusion.1, bf16[16,2,512,128]{3,2,1,0:T(8,128)(2,1)} %bitcast.6.refs_0_.refs_1_.refs_2_.refs_3_.refs_4_.refs_5_.refs_6_.refs_7_, ...), custom_call_target="tpu_custom_call" | custom-call | flops 6710886400 | bytes 4194304 | tf_op jit(solution)/shard_map/pallas_call | solution.py:138
  111.3 0.0 all-gather.3.cloned.1.call-update
  111.3 0.0 all-gather.5.cloned.1.call-start
  111.4 17.6 %all-to-all-done.1 = bf16[8,2,2,512,128]{4,3,2,1,0:T(8,128)(2,1)} async-done(((bf16[8,2,2,512,128]{4,3,2,1,0:T(8,128)(2,1)}), bf16[8,2,2,512,128]{4,3,2,1,0:T(8,128)(2,1)}, u32[]{:S(2)}, u32[]{:S(2)}) %all-to-all-start.1) | async-done | bytes 4194336 | tf_op jit(solution)/shard_map/all_to_all | solution.py:225
  128.9 31.2 %shard_map.110 = bf16[640,512]{1,0:T(8,128)(2,1)} custom-call(s32[16]{0:T(128)S(1)} %fusion.10.slots, s32[16]{0:T(128)S(1)} %gather_fusion.1, bf16[16,2,512,128]{3,2,1,0:T(8,128)(2,1)} %bitcast.10.refs_0_.refs_1_.refs_2_.refs_3_.refs_4_.refs_5_.refs_6_.refs_7_, ...), custom_call_target="tpu_custom_call" | custom-call | flops 6710886400 | bytes 4194304 | tf_op jit(solution)/shard_map/pallas_call | solution.py:138
  160.2 0.0 all-gather.5.cloned.1.call-update
  160.2 5.9 %fusion.11 = (bf16[4,1,512,1024]{3,2,1,0:T(8,128)(2,1)}, bf16[4,1,512,1024]{3,2,1,0:T(8,128)(2,1)}) fusion(bf16[4,2,512,1024]{3,2,1,0:T(8,128)(2,1)} %bitcast.35), kind=kLoop, calls=%fused_computation.42 | loop fusion | bytes 16777216 | tf_op jit(solution)/shard_map/slice | solution.py:247
  166.2 2.2 all-gather.3.cloned.1.call-done
  168.4 7.3 %fusion.13 = f32[640,1024]{1,0:T(8,128)} fusion(bf16[640,2048]{1,0:T(8,128)(2,1)} %all-gather.3.cloned.1.call-done, bf16[2048,1024]{1,0:T(8,128)(2,1)} %bitcast.40), kind=kOutput, calls=%fused_computation.44 | convolution fusion | flops 2684354560 | bytes 9437184 | tf_op jit(solution)/shard_map/dot_general | solution.py:248
  175.7 47.9 %all-gather.5.cloned.1.call-done = bf16[640,2048]{1,0:T(8,128)(2,1)} async-done(((bf16[640,512]{1,0:T(8,128)(2,1)}), bf16[640,2048]{1,0:T(8,128)(2,1)}) %all-gather.5.cloned.1.call-update) | async-done | bytes 2621456 | tf_op jit(solution)/shard_map/all_gather | solution.py:246
  223.6 0.0 copy-start.1
  223.6 7.8 %add_convert_fusion = bf16[640,1024]{1,0:T(8,128)(2,1)} fusion(f32[640,1024]{1,0:T(8,128)} %fusion.13, bf16[640,2048]{1,0:T(8,128)(2,1)} %all-gather.5.cloned.1.call-done, bf16[2048,1024]{1,0:T(8,128)(2,1)} %bitcast.39), kind=kOutput, calls=%fused_computation.9 | convolution fusion | flops 2685665280 | bytes 10747904 | tf_op jit(solution)/shard_map/dot_general | solution.py:248
  231.4 0.0 copy-done.1
  (12 shorter events, 0.1 us)
Async XLA Ops:
  6.5 33.8 %copy-start = (bf16[4096,256]{1,0:T(8,128)(2,1)S(1)}, bf16[4096,256]{1,0:T(8,128)(2,1)}, u32[]{:S(2)}) copy-start(bf16[4096,256]{1,0:T(8,128)(2,1)} %param.15) | copy-start | bytes 6291460
  6.5 1.0 copy-start.2
  20.7 5.3 %copy-start.5 = (s32[16,8]{0,1:T(8,128)S(1)}, s32[16,8]{0,1:T(8,128)}, u32[]{:S(2)}) copy-start(s32[16,8]{0,1:T(8,128)} %param.19) | copy-start | bytes 1540
  20.7 5.4 %copy-start.6 = (s32[2,320]{1,0:T(2,128)S(1)}, s32[2,320]{1,0:T(2,128)}, u32[]{:S(2)}) copy-start(s32[2,320]{1,0:T(2,128)} %param.21) | copy-start | bytes 7684
  20.7 54.5 %all-to-all-start = ((bf16[8,2,2,512,128]{4,3,2,1,0:T(8,128)(2,1)}), bf16[8,2,2,512,128]{4,3,2,1,0:T(8,128)(2,1)}, u32[]{:S(2)}, u32[]{:S(2)}) async-start(bf16[8,2,2,512,128]{4,3,2,1,0:T(8,128)(2,1)} %bitcast.34), calls=%async_computation | async-start | bytes 8388608 | tf_op jit(solution)/shard_map/all_to_all | solution.py:225
  31.6 3.7 %copy-start.3 = (s32[128]{0:T(128)S(1)}, s32[128]{0:T(128)}, u32[]{:S(2)}) copy-start(s32[128]{0:T(128)} %param.20) | copy-start | bytes 1540
  31.6 4.4 %copy-start.4 = (f32[4096]{0:T(1024)S(1)}, f32[4096]{0:T(1024)}, u32[]{:S(2)}) copy-start(f32[4096]{0:T(1024)} %param.12) | copy-start | bytes 49156
  40.4 1.6 copy-start.7
  40.4 3.1 %slice-start = ((s8[8388608]{0:T(1024)(128)(4,1)}), s8[4194304]{0:T(1024)(128)(4,1)S(1)}, s32[]{:S(2)}) async-start(s8[8388608]{0:T(1024)(128)(4,1)} %bitcast.41), calls=%async_computation.4 | async-start | bytes 8388608
  42.0 2.7 %slice-start.1 = ((s8[8388608]{0:T(1024)(128)(4,1)}), s8[4194304]{0:T(1024)(128)(4,1)S(1)}, s32[]{:S(2)}) async-start(s8[8388608]{0:T(1024)(128)(4,1)} %bitcast.41), calls=%async_computation.5 | async-start | bytes 8388608
  75.2 53.7 %all-to-all-start.1 = ((bf16[8,2,2,512,128]{4,3,2,1,0:T(8,128)(2,1)}), bf16[8,2,2,512,128]{4,3,2,1,0:T(8,128)(2,1)}, u32[]{:S(2)}, u32[]{:S(2)}) async-start(bf16[8,2,2,512,128]{4,3,2,1,0:T(8,128)(2,1)} %bitcast.33), calls=%async_computation.1 | async-start | bytes 8388608 | tf_op jit(solution)/shard_map/all_to_all | solution.py:225
  79.8 88.5 %all-gather.3.cloned.1.call-start = ((), (), s32[]{:S(2)}) async-start(), calls=%async_computation.2 | async-start | bytes 3276800 | tf_op jit(solution)/shard_map/all_gather | solution.py:246
  111.3 112.2 %all-gather.5.cloned.1.call-start = ((), (), s32[]{:S(2)}) async-start(), calls=%async_computation.3 | async-start | bytes 3276800 | tf_op jit(solution)/shard_map/all_gather | solution.py:246
  223.6 7.8 %copy-start.1 = (bf16[4096,256]{1,0:T(8,128)(2,1)S(1)}, bf16[4096,256]{1,0:T(8,128)(2,1)}, u32[]{:S(2)}) copy-start(bf16[4096,256]{1,0:T(8,128)(2,1)} %param.15) | copy-start | bytes 6291460
Sparse Core Ops, SparseCore 0:
  111.4 56.8 all-gather.2
  169.9 53.5 all-gather.4
where the time goes:
time: 239 us; the launch traced here: 238 us
  waiting for transfers between devices  92.6 us (39%)
  Pallas kernels  62.5 us (26%)
  local copies, waits for them, and re-layouts  26.2 us (11%)
  matrix products  23.9 us (10%)
  between operations  13.6 us (6%)
  starting transfers between devices  10.2 us (4%)
  other arithmetic  9.35 us (4%)
    pallas_call x2, Pallas kernels, attention(): pl.pallas_call(functools.partial(attention_kernel, retrieved, doc_rows, t...  62.5 us
    all_gather x2, waiting for transfers between devices, body(): gathered = lax.all_gather(attn, 'tp', axis=1, tiled=True)  50.1 us
    all_to_all x2, waiting for transfers between devices, body(): lax.all_to_all(outgoing, 'grp', split_axis=0, concat_axis=0, tiled=True)  42.5 us
    dot_general x2, matrix products, body(): mixed = mixed + jnp.dot(gathered, part, preferred_element_type=jnp.float32)  15.2 us
    gather x2, local copies, waits for them, and re-layouts, body(): outgoing = doc_cache[:, :, :, head * HD:(head + 1) * HD][chosen]  10.4 us
    all_to_all x2, starting transfers between devices, body(): lax.all_to_all(outgoing, 'grp', split_axis=0, concat_axis=0, tiled=True)  9.89 us
    slice x1, local copies, waits for them, and re-layouts, body(): outgoing = doc_cache[:, :, :, head * HD:(head + 1) * HD][chosen]  5.95 us
    slice x1, local copies, waits for them, and re-layouts, body(): part = w_heads[:, head].reshape(-1, w_out.shape[1])  5.94 us
  transfers between devices with their start and end apart: 4, of which 4 were waited for; matrix products, arithmetic and copies ran while one was open for 15% of the time, Pallas kernels for 26%

commit v1 on v0

v1 whole, which is shorter than its diff:
```python
import functools

import jax
import jax.numpy as jnp
from jax import lax
from jax.experimental import pallas as pl
from jax.experimental.pallas import tpu as pltpu
from jax.sharding import PartitionSpec as P

H = 32
KVH = 8
HD = 128
CAP = 2
PAIR = 2
LANES = 128
MASKED = -1e30
LOG2E = 1.4426950408889634


def pick_kernel(chosen, cache, out):
    out[...] = cache[...]


def pick(head, chosen, doc_cache):
    doc_rows = doc_cache.shape[2]
    count = chosen.shape[0]
    return pl.pallas_call(
        pick_kernel,
        grid_spec=pltpu.PrefetchScalarGridSpec(
            num_scalar_prefetch=1,
            grid=(count,),
            in_specs=[pl.BlockSpec((1, 2, doc_rows, HD), lambda i, chosen: (chosen[i], 0, 0, head))],
            out_specs=pl.BlockSpec((1, 2, doc_rows, HD), lambda i, chosen: (i, 0, 0, 0)),
        ),
        out_shape=jax.ShapeDtypeStruct((count, 2, doc_rows, HD), doc_cache.dtype),
        compiler_params=pltpu.CompilerParams(vmem_limit_bytes=32 * 2**20),
        cost_estimate=pl.CostEstimate(
            flops=0, bytes_accessed=8 * count * doc_rows * HD, transcendentals=0
        ),
    )(chosen, doc_cache)


def place_kernel(retrieved, doc_rows, new_k, new_v, pos_lane, keep, *placed):
    tokens = new_k.shape[0]
    picks = tokens // retrieved
    for j in range(retrieved):
        low = j * picks // LANES * LANES
        high = min(tokens, -(-(j + 1) * picks // LANES) * LANES)
        at = lax.broadcasted_iota(jnp.int32, (doc_rows, high - low), 0) + j * doc_rows
        hit = jnp.where(at == pos_lane[0, :, low:high], 1.0, 0.0).astype(jnp.bfloat16)
        ones = jnp.ones((high - low, HD), jnp.bfloat16)
        taken = jnp.dot(hit, ones, preferred_element_type=jnp.float32)
        keep[j] = (1.0 - taken).astype(jnp.bfloat16)
        for head, out in enumerate(placed):
            cols = slice(head * HD, (head + 1) * HD)
            for n, fresh in enumerate((new_k, new_v)):
                out[j, n] = jnp.dot(
                    hit, fresh[low:high, cols], preferred_element_type=jnp.float32
                ).astype(jnp.bfloat16)


def place(doc_rows, retrieved, key_new, value_new, positions):
    served, tokens = positions.shape
    width = key_new.shape[1]
    heads = width // HD
    count = served * retrieved
    placed = jax.ShapeDtypeStruct((count, 2, doc_rows, HD), jnp.bfloat16)
    return pl.pallas_call(
        functools.partial(place_kernel, retrieved, doc_rows),
        grid=(served,),
        in_specs=[
            pl.BlockSpec((tokens, width), lambda r: (r, 0)),
            pl.BlockSpec((tokens, width), lambda r: (r, 0)),
            pl.BlockSpec((1, 1, tokens), lambda r: (r, 0, 0)),
        ],
        out_specs=[pl.BlockSpec((retrieved, doc_rows, HD), lambda r: (r, 0, 0))]
        + [pl.BlockSpec((retrieved, 2, doc_rows, HD), lambda r: (r, 0, 0, 0))] * heads,
        out_shape=[jax.ShapeDtypeStruct((count, doc_rows, HD), jnp.bfloat16)] + [placed] * heads,
        compiler_params=pltpu.CompilerParams(vmem_limit_bytes=40 * 2**20),
        cost_estimate=pl.CostEstimate(
            flops=2 * count * doc_rows * 256 * (2 * heads + 1) * HD,
            bytes_accessed=2 * count * doc_rows * (2 * heads + 1) * HD,
            transcendentals=0,
        ),
    )(key_new, value_new, positions[:, None, :])


def attention_kernel(retrieved, doc_rows, tokens, first_doc, slots, lens, *refs):
    docs = refs[:retrieved]
    q_ref, keep, placed, pos_col, o_ref = refs[retrieved : retrieved + 5]
    keys, values, scores, top, total, acc = refs[retrieved + 5 :]
    group = H // KVH
    picks = tokens // retrieved
    span = PAIR * picks
    wide = PAIR * doc_rows
    per_doc = doc_rows // LANES
    factor = HD ** (-0.5) * LOG2E
    block = pl.program_id(0)

    @pl.when(block == 0)
    def blend():
        for j in range(retrieved):
            rows = slice(j * doc_rows, (j + 1) * doc_rows)
            keys[rows, :] = docs[j][0, 0] * keep[j] + placed[j, 0]
            values[rows, :] = docs[j][0, 1] * keep[j] + placed[j, 1]

    top[...] = jnp.full_like(top, MASKED)
    total[...] = jnp.zeros_like(total)
    acc[...] = jnp.zeros_like(acc)
    lane = lax.broadcasted_iota(jnp.int32, (span, LANES), 1)
    half = group // 2
    first_heads = tuple(range(half))
    second_heads = tuple(range(half, group))

    def rows_of(g):
        return slice(g * span, (g + 1) * span)

    def some(heads):
        return slice(heads[0] * span, (heads[-1] + 1) * span)

    def columns_of(n):
        return slice(n * LANES, (n + 1) * LANES)

    def context(ref, p):
        return ref[pl.ds(pl.multiple_of(p * wide, wide), wide), :]

    def score(p, heads):
        query = jnp.concatenate([q_ref[:, columns_of(g)] for g in heads], axis=0)
        raw = lax.dot_general(
            query, context(keys, p), (((1,), (1,)), ((), ())), preferred_element_type=jnp.float32
        )
        limits = []
        for n in range(PAIR):
            doc = p * PAIR + n
            limit = jnp.minimum(pos_col[...] - doc * doc_rows, lens[first_doc + doc] - 1)
            limits.append(jnp.broadcast_to(limit, (span, LANES)))
        best = [top[rows_of(g), :] for g in heads]
        for n in range(wide // LANES):
            mask = lane + (n % per_doc) * LANES <= limits[n // per_doc]
            for at, g in enumerate(heads):
                part = jnp.where(mask, raw[at * span : (at + 1) * span, columns_of(n)], MASKED)
                scores[p, rows_of(g), columns_of(n)] = part
                best[at] = jnp.maximum(best[at], part)
        for at, g in enumerate(heads):
            top[rows_of(g), :] = best[at]

    def settle_top(heads):
        rows = some(heads)
        peak = jnp.max(top[rows, :], axis=1, keepdims=True) * factor
        top[rows, :] = jnp.broadcast_to(peak, (len(heads) * span, LANES))

    def exponent(p, heads):
        for g in heads:
            rows = rows_of(g)
            shift = top[rows, :]
            add = total[rows, :]
            for n in range(wide // LANES):
                expo = jnp.exp2(scores[p, rows, columns_of(n)] * factor - shift)
                scores[p, rows, columns_of(n)] = expo
                add = add + expo
            total[rows, :] = add

    def settle_total(heads):
        rows = some(heads)
        inverse = 1.0 / jnp.sum(total[rows, :], axis=1, keepdims=True)
        total[rows, :] = jnp.broadcast_to(inverse, (len(heads) * span, LANES))

    def combine(p, heads):
        rows = some(heads)
        scale = total[rows, :]
        weights = jnp.concatenate(
            [
                (scores[p, rows, columns_of(n)] * scale).astype(jnp.bfloat16)
                for n in range(wide // LANES)
            ],
            axis=1,
        )
        acc[rows, :] += jnp.dot(weights, context(values, p), preferred_element_type=jnp.float32)

    @pl.loop(0, block + 1)
    def _(p):
        score(p, first_heads)

    settle_top(first_heads)

    @pl.loop(0, block + 1)
    def _(p):
        score(p, second_heads)
        exponent(p, first_heads)

    settle_top(second_heads)
    settle_total(first_heads)

    @pl.loop(0, block + 1)
    def _(p):
        exponent(p, second_heads)
        combine(p, first_heads)

    settle_total(second_heads)

    @pl.loop(0, block + 1)
    def _(p):
        combine(p, second_heads)

    for g in range(group):
        o_ref[:, columns_of(g)] = acc[rows_of(g), :].astype(o_ref.dtype)


def attention(head, request, cache, slots, lens, query, keep, placed, positions):
    served, tokens = positions.shape
    retrieved = slots.shape[0] // served
    doc_rows = cache.shape[2]
    group = H // KVH
    span = tokens // retrieved * PAIR
    blocks = retrieved // PAIR
    rows = group * span
    first_doc = request * retrieved
    doc_specs = [
        pl.BlockSpec(
            (1, 2, doc_rows, HD), lambda b, slots, lens, j=j: (slots[first_doc + j], 0, 0, 0)
        )
        for j in range(retrieved)
    ]
    pairs = tokens * group * retrieved * doc_rows * 5 // 8
    return pl.pallas_call(
        functools.partial(attention_kernel, retrieved, doc_rows, tokens, first_doc),
        grid_spec=pltpu.PrefetchScalarGridSpec(
            num_scalar_prefetch=2,
            grid=(blocks,),
            in_specs=doc_specs
            + [
                pl.BlockSpec((span, group * HD), lambda b, *_: (request * blocks + b, head)),
                pl.BlockSpec((retrieved, doc_rows, HD), lambda b, *_: (request, 0, 0)),
                pl.BlockSpec((retrieved, 2, doc_rows, HD), lambda b, *_: (request, 0, 0, 0)),
                pl.BlockSpec((span, 1), lambda b, *_: (request * blocks + b, 0)),
            ],
            out_specs=pl.BlockSpec((span, group * HD), lambda b, *_: (b, 0)),
            scratch_shapes=[
                pltpu.VMEM((retrieved * doc_rows, HD), jnp.bfloat16),
                pltpu.VMEM((retrieved * doc_rows, HD), jnp.bfloat16),
                pltpu.VMEM((blocks, rows, PAIR * doc_rows), jnp.float32),
                pltpu.VMEM((rows, LANES), jnp.float32),
                pltpu.VMEM((rows, LANES), jnp.float32),
                pltpu.VMEM((rows, HD), jnp.float32),
            ],
        ),
        out_shape=jax.ShapeDtypeStruct((tokens, group * HD), jnp.bfloat16),
        compiler_params=pltpu.CompilerParams(vmem_limit_bytes=48 * 2**20),
        cost_estimate=pl.CostEstimate(
            flops=8 * pairs * HD,
            bytes_accessed=2 * retrieved * doc_rows * 5 * HD,
            transcendentals=pairs,
        ),
    )(
        slots,
        lens,
        *([cache] * retrieved),
        query,
        keep,
        placed,
        positions.reshape(served * tokens, 1),
    )


def body(
    sel_hidden,
    norm_gain,
    w_query,
    w_key,
    w_value,
    w_out,
    doc_cache,
    home,
    doc_ids,
    doc_len,
    positions,
):
    groups = lax.axis_size("grp")
    me = lax.axis_index("grp")
    stored = doc_cache.shape[0]
    doc_rows = doc_cache.shape[2]
    width = doc_cache.shape[3]
    kv_local = width // HD
    group = H // KVH
    served = sel_hidden.shape[0]
    tokens = sel_hidden.shape[1]
    retrieved = doc_ids.shape[1]
    per_group = served * retrieved
    location = home[doc_ids].reshape(groups, per_group)
    owner = location // stored
    slot_index = location % stored
    slots = jnp.arange(per_group, dtype=jnp.int32)
    earlier = (owner[:, :, None] == owner[:, None, :]) & (
        slots[None, None, :] < slots[None, :, None]
    )
    rank = jnp.sum(earlier.astype(jnp.int32), axis=2)
    match = (owner == me)[:, :, None] & (
        rank[:, :, None] == jnp.arange(CAP, dtype=jnp.int32)[None, None, :]
    )
    chosen = jnp.sum(jnp.where(match, slot_index[:, :, None], 0), axis=1)
    own_slots = owner[me] * CAP + rank[me]
    lengths = doc_len[doc_ids.reshape(groups, per_group)[me]]

    incoming = []
    for head in range(kv_local):
        outgoing = pick(head, chosen.reshape(groups * CAP), doc_cache).reshape(
            groups, CAP, 2, doc_rows, HD
        )
        if incoming:
            outgoing, incoming[-1] = lax.optimization_barrier((outgoing, incoming[-1]))
        incoming.append(
            lax.all_to_all(outgoing, "grp", split_axis=0, concat_axis=0, tiled=True)
        )

    xf = sel_hidden.astype(jnp.float32)
    normed = (xf * lax.rsqrt(jnp.mean(xf * xf, axis=-1, keepdims=True) + 1e-05) * norm_gain).astype(
        jnp.bfloat16
    )
    normed_rows = normed.reshape(served * tokens, normed.shape[2])
    query = jnp.dot(normed_rows, w_query, preferred_element_type=jnp.float32).astype(jnp.bfloat16)
    key_new = jnp.dot(normed_rows, w_key, preferred_element_type=jnp.float32).astype(jnp.bfloat16)
    value_new = jnp.dot(normed_rows, w_value, preferred_element_type=jnp.float32).astype(
        jnp.bfloat16
    )

    keep, *placed = place(doc_rows, retrieved, key_new, value_new, positions)
    w_heads = w_out.reshape(-1, kv_local, group * HD, w_out.shape[1])
    mixed = [0.0] * served
    for head in range(kv_local):
        cache = incoming[head].reshape((groups * CAP, 2, doc_rows, HD))
        part = w_heads[:, head].reshape(-1, w_out.shape[1])
        for request in range(served):
            attn = attention(
                head, request, cache, own_slots, lengths, query, keep, placed[head], positions
            )
            gathered = lax.all_gather(attn, "tp", axis=1, tiled=True)
            mixed[request] = mixed[request] + jnp.dot(
                gathered, part, preferred_element_type=jnp.float32
            )
    return jnp.stack(mixed).astype(jnp.bfloat16)


def solution(mesh):
    return jax.shard_map(
        body,
        mesh=mesh,
        in_specs=(
            P("grp", None, None),
            P(),
            P(None, "tp"),
            P(None, "tp"),
            P(None, "tp"),
            P(None, "tp"),
            P("grp", None, None, "tp"),
            P(),
            P(),
            P(),
            P("grp", None),
        ),
        out_specs=P("grp", None, "tp"),
        check_vma=False,
    )
```

time: 239 us -> 242 us (1.013)
  waiting for transfers between devices: 92.6 us -> 71.8 us
  Pallas kernels: 62.5 us -> 73.7 us
  matrix products: 23.9 us -> 30.5 us
  local copies, waits for them, and re-layouts: 26.2 us -> 30.9 us
    unnamed x21 -> x45, local copies, waits for them, and re-layouts: 1.25 us -> 21.6 us
    all_to_all x2, waiting for transfers between devices: 42.5 us -> 25.4 us  [body(): lax.all_to_all(outgoing, 'grp', split_axis=0, concat_axis=0, tiled=True)]
    gather x2 -> x0, local copies, waits for them, and re-layouts: 10.4 us -> none  [body(): outgoing = doc_cache[:, :, :, head * HD:(head + 1) * HD][chosen]]
    pallas_call x0 -> x3, Pallas kernels: none -> 7.35 us  [the longest x1 3.75 us: place(): pl.pallas_call(functools.partial(place_kernel, retrieved, doc_rows), grid...]
    slice x1 -> x0, local copies, waits for them, and re-layouts: 5.95 us -> none  [body(): outgoing = doc_cache[:, :, :, head * HD:(head + 1) * HD][chosen]]
    dot_general x2 -> x4, matrix products: 15.2 us -> 19.6 us  [body(): jnp.dot(gathered, part, preferred_element_type=jnp.float32)]
    pallas_call x2 -> x4, Pallas kernels: 62.5 us -> 66.4 us  [attention(): pl.pallas_call(functools.partial(attention_kernel, retrieved, doc_rows, t...]
    all_gather x2 -> x4, waiting for transfers between devices: 50.1 us -> 46.3 us  [body(): gathered = lax.all_gather(attn, 'tp', axis=1, tiled=True)]
  transfers between devices with their start and end apart: 4 -> 6, of which waited for: 4 -> 4; matrix products, arithmetic and copies ran while one was open for 15% -> 17% of each run, Pallas kernels for 26% -> 30%
where the time goes in v1:
time: 242 us; the launch traced here: 241 us
  Pallas kernels  73.7 us (30%)
  waiting for transfers between devices  71.8 us (30%)
  local copies, waits for them, and re-layouts  30.9 us (13%)
  matrix products  30.5 us (13%)
  between operations  13.4 us (6%)
  other arithmetic  10.7 us (4%)
  starting transfers between devices  10.3 us (4%)
    pallas_call x4, Pallas kernels, attention(): pl.pallas_call(functools.partial(attention_kernel, retrieved, doc_rows, t...  66.4 us
    all_gather x4, waiting for transfers between devices, body(): gathered = lax.all_gather(attn, 'tp', axis=1, tiled=True)  46.3 us
    all_to_all x2, waiting for transfers between devices, body(): lax.all_to_all(outgoing, 'grp', split_axis=0, concat_axis=0, tiled=True)  25.4 us
    unnamed x45, local copies, waits for them, and re-layouts  21.6 us
    dot_general x4, matrix products, body(): jnp.dot(gathered, part, preferred_element_type=jnp.float32)  19.6 us
    all_to_all x2, starting transfers between devices, body(): lax.all_to_all(outgoing, 'grp', split_axis=0, concat_axis=0, tiled=True)  9.96 us
    dot_general x1, matrix products, body(): jnp.dot(normed_rows, w_query, preferred_element_type=jnp.float32)  7.95 us
    slice x1, local copies, waits for them, and re-layouts, body(): part = w_heads[:, head].reshape(-1, w_out.shape[1])  5.97 us
  transfers between devices with their start and end apart: 6, of which 4 were waited for; matrix products, arithmetic and copies ran while one was open for 17% of the time, Pallas kernels for 30%

profile of v1, /device:TPU:0, one launch (start us, length us, event | category | flops | bytes accessed | tf_op | source)
XLA Modules:
  0.0 241.3 jit_solution(4712048755002303778)
XLA Ops:
  6.6 0.8 compare_select_fusion
  7.4 0.1 copy.20
  7.5 0.1 reshape.189
  7.6 1.2 gather_fusion
  8.8 0.1 reshape.177
  8.9 0.3 convert_reduce_fusion
  9.2 0.2 select_reduce_fusion
  9.4 0.1 copy.22
  9.4 0.1 reshape.179.chosen
  9.5 3.4 %copy-done.2 = bf16[16,2,512,256]{3,2,1,0:T(8,128)(2,1)S(1)} copy-done((bf16[16,2,512,256]{3,2,1,0:T(8,128)(2,1)S(1)}, bf16[16,2,512,256]{3,2,1,0:T(8,128)(2,1)}, u32[]{:S(2)}) %copy-start.2) | copy-done | bytes 8388632
  12.9 1.8 shard_map.110
  14.7 2.0 copy-done.7
  16.7 5.4 %all-to-all-start = ((bf16[8,2,2,512,128]{4,3,2,1,0:T(8,128)(2,1)}), bf16[8,2,2,512,128]{4,3,2,1,0:T(8,128)(2,1)}, u32[]{:S(2)}, u32[]{:S(2)}) async-start(bf16[8,2,2,512,128]{4,3,2,1,0:T(8,128)(2,1)} %bitcast.37), calls=%async_computation | async-start | bytes 8388608 | tf_op jit(solution)/shard_map/all_to_all | solution.py:312
  22.1 0.1 copy.21
  22.2 1.0 reshape.206.refs_11_
  23.2 3.4 %copy-done.3 = bf16[16,2,512,256]{3,2,1,0:T(8,128)(2,1)S(1)} copy-done((bf16[16,2,512,256]{3,2,1,0:T(8,128)(2,1)S(1)}, bf16[16,2,512,256]{3,2,1,0:T(8,128)(2,1)}, u32[]{:S(2)}) %copy-start.3) | copy-done | bytes 8388632
  26.6 1.8 shard_map.109
  28.4 2.0 copy-done.6
  30.4 3.6 %fusion = f32[2,320]{1,0:T(2,128)S(1)} fusion(bf16[2,320,4096]{2,1,0:T(8,128)(2,1)} %param.11), kind=kLoop, calls=%fused_computation.4 | loop fusion | flops 7863680 | bytes 5245440 | tf_op jit(solution)/shard_map/reduce_sum | solution.py:316
  34.0 0.1 reshape.178
  34.1 0.7 gather_fusion.1
  34.8 4.5 %fusion.2 = bf16[2,320,4096]{2,1,0:T(8,128)(2,1)S(1)} fusion(bf16[2,320,4096]{2,1,0:T(8,128)(2,1)} %param.11, f32[4096]{0:T(1024)S(1)} %copy-done.18, f32[2,320]{1,0:T(2,128)S(1)} %add_rsqrt_fusion), kind=kLoop, calls=%fused_computation.6 | loop fusion | flops 10485760 | bytes 10504704 | tf_op jit(solution)/shard_map/convert_element_type | solution.py:316
  39.4 0.0 copy-start.21
  39.4 1.5 convolution_convert_fusion.1.new_v
  40.9 0.1 copy-done.21
  41.0 1.5 convolution_convert_fusion.2.new_k
  42.5 3.8 %shard_map.111 = (bf16[16,512,128]{2,1,0:T(8,128)(2,1)S(1)}, bf16[16,2,512,128]{3,2,1,0:T(8,128)(2,1)S(1)}, bf16[16,2,512,128]{3,2,1,0:T(8,128)(2,1)S(1)}) custom-call(bf16[640,256]{1,0:T(8,128)(2,1)S(1)} %convolution_convert_fusion.2.new_k, bf16[640,256]{1,0:T(8,128)(2,1)S(1)} %convolution_convert_fusion.1.new_v, s32[2,1,320]{2,1,0:T(1,128)S(1)} %broadcast_in_dim.19.pos_lane), custom_call_target="tpu_custom_call" | custom-call | flops 2684354560 | bytes 10485760 | tf_op jit(solution)/shard_map/pallas_call | solution.py:68
  46.2 2.0 copy-done.4
  48.2 2.0 copy-done.5
  50.2 7.9 %convolution_convert_fusion.refs_8_ = bf16[640,1024]{1,0:T(8,128)(2,1)S(1)} fusion(bf16[640,4096]{1,0:T(8,128)(2,1)S(1)} %bitcast.41, bf16[4096,1024]{1,0:T(8,128)(2,1)} %param.13), kind=kOutput, calls=%fused_computation.7 | convolution fusion | flops 5369364480 | bytes 14942208 | tf_op jit(solution)/shard_map/dot_general | solution.py:320
  58.1 13.2 %all-to-all-done = bf16[8,2,2,512,128]{4,3,2,1,0:T(8,128)(2,1)} async-done(((bf16[8,2,2,512,128]{4,3,2,1,0:T(8,128)(2,1)}), bf16[8,2,2,512,128]{4,3,2,1,0:T(8,128)(2,1)}, u32[]{:S(2)}, u32[]{:S(2)}) %all-to-all-start) | async-done | bytes 4194336 | tf_op jit(solution)/shard_map/all_to_all | solution.py:312
  71.4 4.6 %all-to-all-start.1 = ((bf16[8,2,2,512,128]{4,3,2,1,0:T(8,128)(2,1)}), bf16[8,2,2,512,128]{4,3,2,1,0:T(8,128)(2,1)}, u32[]{:S(2)}, u32[]{:S(2)}) async-start(bf16[8,2,2,512,128]{4,3,2,1,0:T(8,128)(2,1)} %bitcast.36), calls=%async_computation.1 | async-start | bytes 8388608 | tf_op jit(solution)/shard_map/all_to_all | solution.py:312
  75.9 0.2 all-gather.5.cloned.1.call-start
  76.2 0.0 copy-start.8
  76.2 1.0 copy-done.8
  77.1 16.6 %shard_map.112 = bf16[320,512]{1,0:T(8,128)(2,1)S(1)} custom-call(s32[16]{0:T(128)S(1)} %fusion.14.slots, s32[16]{0:T(128)S(1)} %gather_fusion.1, bf16[16,2,512,128]{3,2,1,0:T(8,128)(2,1)} %bitcast.5.refs_0_.refs_1_.refs_2_.refs_3_.refs_4_.refs_5_.refs_6_.refs_7_, ...), custom_call_target="tpu_custom_call" | custom-call | flops 3355443200 | bytes 5242880 | tf_op jit(solution)/shard_map/pallas_call | solution.py:225
  93.7 0.7 copy-done.12
  94.5 0.0 all-gather.5.cloned.1.call-update
  94.5 0.0 all-gather.9.cloned.1.call-start
  94.5 0.0 copy-start.9
  94.5 1.0 copy-done.9
  95.5 16.6 %shard_map.114 = bf16[320,512]{1,0:T(8,128)(2,1)S(1)} custom-call(s32[16]{0:T(128)S(1)} %fusion.14.slots, s32[16]{0:T(128)S(1)} %gather_fusion.1, bf16[16,2,512,128]{3,2,1,0:T(8,128)(2,1)} %bitcast.5.refs_0_.refs_1_.refs_2_.refs_3_.refs_4_.refs_5_.refs_6_.refs_7_, ...), custom_call_target="tpu_custom_call" | custom-call | flops 3355443200 | bytes 5242880 | tf_op jit(solution)/shard_map/pallas_call | solution.py:225
  112.1 0.7 copy-done.13
  112.8 0.0 all-gather.9.cloned.1.call-update
  112.9 0.0 all-gather.7.cloned.1.call-start
  112.9 12.2 %all-to-all-done.1 = bf16[8,2,2,512,128]{4,3,2,1,0:T(8,128)(2,1)} async-done(((bf16[8,2,2,512,128]{4,3,2,1,0:T(8,128)(2,1)}), bf16[8,2,2,512,128]{4,3,2,1,0:T(8,128)(2,1)}, u32[]{:S(2)}, u32[]{:S(2)}) %all-to-all-start.1) | async-done | bytes 4194336 | tf_op jit(solution)/shard_map/all_to_all | solution.py:312
  125.1 1.0 copy-done.10
  126.0 16.6 %shard_map.113 = bf16[320,512]{1,0:T(8,128)(2,1)S(1)} custom-call(s32[16]{0:T(128)S(1)} %fusion.14.slots, s32[16]{0:T(128)S(1)} %gather_fusion.1, bf16[16,2,512,128]{3,2,1,0:T(8,128)(2,1)} %bitcast.9.refs_0_.refs_1_.refs_2_.refs_3_.refs_4_.refs_5_.refs_6_.refs_7_, ...), custom_call_target="tpu_custom_call" | custom-call | flops 3355443200 | bytes 5242880 | tf_op jit(solution)/shard_map/pallas_call | solution.py:225
  142.6 0.7 copy-done.14
  143.4 0.0 all-gather.7.cloned.1.call-update
  143.4 0.0 all-gather.11.cloned.1.call-start
  143.4 0.0 copy-start.11
  143.5 1.0 copy-done.11
  144.4 16.6 %shard_map.115 = bf16[320,512]{1,0:T(8,128)(2,1)S(1)} custom-call(s32[16]{0:T(128)S(1)} %fusion.14.slots, s32[16]{0:T(128)S(1)} %gather_fusion.1, bf16[16,2,512,128]{3,2,1,0:T(8,128)(2,1)} %bitcast.9.refs_0_.refs_1_.refs_2_.refs_3_.refs_4_.refs_5_.refs_6_.refs_7_, ...), custom_call_target="tpu_custom_call" | custom-call | flops 3355443200 | bytes 5242880 | tf_op jit(solution)/shard_map/pallas_call | solution.py:225
  161.1 0.7 copy-done.15
  161.8 0.0 all-gather.11.cloned.1.call-update
  161.8 6.0 %fusion.15 = (bf16[4,1,512,1024]{3,2,1,0:T(8,128)(2,1)}, bf16[4,1,512,1024]{3,2,1,0:T(8,128)(2,1)}) fusion(bf16[4,2,512,1024]{3,2,1,0:T(8,128)(2,1)} %bitcast.38), kind=kLoop, calls=%fused_computation.44 | loop fusion | bytes 16777216 | tf_op jit(solution)/shard_map/slice | solution.py:331
  167.8 5.3 %fusion.16 = f32[320,1024]{1,0:T(8,128)} fusion(bf16[320,2048]{1,0:T(8,128)(2,1)} %all-gather.5.cloned.1.call-done, bf16[2048,1024]{1,0:T(8,128)(2,1)} %bitcast.44), kind=kOutput, calls=%fused_computation.45 | convolution fusion | flops 1342177280 | bytes 6815744 | tf_op jit(solution)/shard_map/dot_general | solution.py:337
  173.0 5.2 %fusion.17 = f32[320,1024]{1,0:T(8,128)} fusion(bf16[320,2048]{1,0:T(8,128)(2,1)} %all-gather.9.cloned.1.call-done, bf16[2048,1024]{1,0:T(8,128)(2,1)} %bitcast.45), kind=kOutput, calls=%fused_computation.46 | convolution fusion | flops 1342177280 | bytes 6815744 | tf_op jit(solution)/shard_map/dot_general | solution.py:337
  178.2 17.8 %all-gather.7.cloned.1.call-done = bf16[320,2048]{1,0:T(8,128)(2,1)} async-done(((bf16[320,512]{1,0:T(8,128)(2,1)}), bf16[320,2048]{1,0:T(8,128)(2,1)}) %all-gather.7.cloned.1.call-update) | async-done | bytes 1310736 | tf_op jit(solution)/shard_map/all_gather | solution.py:336
  196.0 4.6 %fusion.6 = bf16[1,320,1024]{2,1,0:T(8,128)(2,1)S(1)} fusion(f32[320,1024]{1,0:T(8,128)} %fusion.16, bf16[320,2048]{1,0:T(8,128)(2,1)} %all-gather.7.cloned.1.call-done, bf16[2048,1024]{1,0:T(8,128)(2,1)} %bitcast.42), kind=kOutput, calls=%fused_computation.14 | convolution fusion | flops 1342832640 | bytes 7471104 | tf_op jit(solution)/shard_map/dot_general | solution.py:337
  200.6 28.5 %all-gather.11.cloned.1.call-done = bf16[320,2048]{1,0:T(8,128)(2,1)} async-done(((bf16[320,512]{1,0:T(8,128)(2,1)}), bf16[320,2048]{1,0:T(8,128)(2,1)}) %all-gather.11.cloned.1.call-update) | async-done | bytes 1310736 | tf_op jit(solution)/shard_map/all_gather | solution.py:336
  229.2 4.5 %fusion.5 = bf16[1,320,1024]{2,1,0:T(8,128)(2,1)S(1)} fusion(f32[320,1024]{1,0:T(8,128)} %fusion.17, bf16[320,2048]{1,0:T(8,128)(2,1)} %all-gather.11.cloned.1.call-done, bf16[2048,1024]{1,0:T(8,128)(2,1)} %bitcast.43), kind=kOutput, calls=%fused_computation.13 | convolution fusion | flops 1342832640 | bytes 7471104 | tf_op jit(solution)/shard_map/dot_general | solution.py:337
  233.6 1.2 pad_maximum_fusion
  (36 shorter events, 0.1 us)
Async XLA Ops:
  6.5 32.8 %copy-start = (bf16[4096,256]{1,0:T(8,128)(2,1)S(1)}, bf16[4096,256]{1,0:T(8,128)(2,1)}, u32[]{:S(2)}) copy-start(bf16[4096,256]{1,0:T(8,128)(2,1)} %param.15) | copy-start | bytes 6291460
  6.5 1.0 copy-start.16
  9.5 3.4 %copy-start.2 = (bf16[16,2,512,256]{3,2,1,0:T(8,128)(2,1)S(1)}, bf16[16,2,512,256]{3,2,1,0:T(8,128)(2,1)}, u32[]{:S(2)}) copy-start(bf16[16,2,512,256]{3,2,1,0:T(8,128)(2,1)} %cache.3) | copy-start | bytes 25165828
  14.7 2.0 copy-start.7
  16.7 5.4 %copy-start.19 = (s32[16,8]{0,1:T(8,128)S(1)}, s32[16,8]{0,1:T(8,128)}, u32[]{:S(2)}) copy-start(s32[16,8]{0,1:T(8,128)} %param.19) | copy-start | bytes 1540
  16.7 5.5 %copy-start.20 = (s32[2,320]{1,0:T(2,128)S(1)}, s32[2,320]{1,0:T(2,128)}, u32[]{:S(2)}) copy-start(s32[2,320]{1,0:T(2,128)} %param.21) | copy-start | bytes 7684
  16.7 54.6 %all-to-all-start = ((bf16[8,2,2,512,128]{4,3,2,1,0:T(8,128)(2,1)}), bf16[8,2,2,512,128]{4,3,2,1,0:T(8,128)(2,1)}, u32[]{:S(2)}, u32[]{:S(2)}) async-start(bf16[8,2,2,512,128]{4,3,2,1,0:T(8,128)(2,1)} %bitcast.37), calls=%async_computation | async-start | bytes 8388608 | tf_op jit(solution)/shard_map/all_to_all | solution.py:312
  23.2 3.4 %copy-start.3 = (bf16[16,2,512,256]{3,2,1,0:T(8,128)(2,1)S(1)}, bf16[16,2,512,256]{3,2,1,0:T(8,128)(2,1)}, u32[]{:S(2)}) copy-start(bf16[16,2,512,256]{3,2,1,0:T(8,128)(2,1)} %cache.3) | copy-start | bytes 25165828
  28.4 2.0 copy-start.6
  30.4 3.7 %copy-start.17 = (s32[128]{0:T(128)S(1)}, s32[128]{0:T(128)}, u32[]{:S(2)}) copy-start(s32[128]{0:T(128)} %param.20) | copy-start | bytes 1540
  30.4 4.4 %copy-start.18 = (f32[4096]{0:T(1024)S(1)}, f32[4096]{0:T(1024)}, u32[]{:S(2)}) copy-start(f32[4096]{0:T(1024)} %param.12) | copy-start | bytes 49156
  39.4 1.6 copy-start.21
  46.2 2.0 copy-start.4
  48.2 2.0 copy-start.5
  71.4 53.7 %all-to-all-start.1 = ((bf16[8,2,2,512,128]{4,3,2,1,0:T(8,128)(2,1)}), bf16[8,2,2,512,128]{4,3,2,1,0:T(8,128)(2,1)}, u32[]{:S(2)}, u32[]{:S(2)}) async-start(bf16[8,2,2,512,128]{4,3,2,1,0:T(8,128)(2,1)} %bitcast.36), calls=%async_computation.1 | async-start | bytes 8388608 | tf_op jit(solution)/shard_map/all_to_all | solution.py:312
  75.9 91.8 %all-gather.5.cloned.1.call-start = ((), (), s32[]{:S(2)}) async-start(), calls=%async_computation.2 | async-start | bytes 1638400 | tf_op jit(solution)/shard_map/all_gather | solution.py:336
  76.2 1.0 copy-start.8
  93.7 0.7 copy-start.12
  94.5 78.6 %all-gather.9.cloned.1.call-start = ((), (), s32[]{:S(2)}) async-start(), calls=%async_computation.4 | async-start | bytes 1638400 | tf_op jit(solution)/shard_map/all_gather | solution.py:336
  94.5 1.0 copy-start.9
  112.1 0.7 copy-start.13
  112.9 83.1 %all-gather.7.cloned.1.call-start = ((), (), s32[]{:S(2)}) async-start(), calls=%async_computation.3 | async-start | bytes 1638400 | tf_op jit(solution)/shard_map/all_gather | solution.py:336
  125.1 1.0 copy-start.10
  142.6 0.8 copy-start.14
  143.4 85.8 %all-gather.11.cloned.1.call-start = ((), (), s32[]{:S(2)}) async-start(), calls=%async_computation.5 | async-start | bytes 1638400 | tf_op jit(solution)/shard_map/all_gather | solution.py:336
  143.4 1.0 copy-start.11
  161.0 0.7 copy-start.15
  196.0 38.8 %copy-start.1 = (bf16[4096,256]{1,0:T(8,128)(2,1)S(1)}, bf16[4096,256]{1,0:T(8,128)(2,1)}, u32[]{:S(2)}) copy-start(bf16[4096,256]{1,0:T(8,128)(2,1)} %param.15) | copy-start | bytes 6291460
Sparse Core Ops, SparseCore 0:
  94.6 34.7 all-gather.4
  131.0 31.6 all-gather.8
  164.3 31.6 all-gather.6
  197.4 31.6 all-gather.10

commit v2 on v1

v2 whole, which is shorter than its diff:
```python
import functools

import jax
import jax.numpy as jnp
from jax import lax
from jax.experimental import pallas as pl
from jax.experimental.pallas import tpu as pltpu
from jax.sharding import PartitionSpec as P

H = 32
KVH = 8
HD = 128
CAP = 2
PAIR = 2
LANES = 128
MASKED = -1e30
VMEM_GRANT = 54 * 2**20
LOG2E = 1.4426950408889634


def pick_kernel(chosen, cache, out):
    out[...] = cache[...]


def pick(head, chosen, doc_cache):
    doc_rows = doc_cache.shape[2]
    count = chosen.shape[0]
    return pl.pallas_call(
        pick_kernel,
        grid_spec=pltpu.PrefetchScalarGridSpec(
            num_scalar_prefetch=1,
            grid=(count,),
            in_specs=[pl.BlockSpec((1, 2, doc_rows, HD), lambda i, chosen: (chosen[i], 0, 0, head))],
            out_specs=pl.BlockSpec((1, 2, doc_rows, HD), lambda i, chosen: (i, 0, 0, 0)),
        ),
        out_shape=jax.ShapeDtypeStruct((count, 2, doc_rows, HD), doc_cache.dtype),
        compiler_params=pltpu.CompilerParams(vmem_limit_bytes=VMEM_GRANT),
        cost_estimate=pl.CostEstimate(
            flops=0, bytes_accessed=8 * count * doc_rows * HD, transcendentals=0
        ),
    )(chosen, doc_cache)


def place_kernel(retrieved, doc_rows, new_k, new_v, pos_lane, keep, *placed):
    tokens = new_k.shape[0]
    picks = tokens // retrieved
    for j in range(retrieved):
        low = j * picks // LANES * LANES
        high = min(tokens, -(-(j + 1) * picks // LANES) * LANES)
        at = lax.broadcasted_iota(jnp.int32, (doc_rows, high - low), 0) + j * doc_rows
        hit = jnp.where(at == pos_lane[0, :, low:high], 1.0, 0.0).astype(jnp.bfloat16)
        ones = jnp.ones((high - low, HD), jnp.bfloat16)
        taken = jnp.dot(hit, ones, preferred_element_type=jnp.float32)
        keep[j] = (1.0 - taken).astype(jnp.bfloat16)
        for head, out in enumerate(placed):
            cols = slice(head * HD, (head + 1) * HD)
            for n, fresh in enumerate((new_k, new_v)):
                out[j, n] = jnp.dot(
                    hit, fresh[low:high, cols], preferred_element_type=jnp.float32
                ).astype(jnp.bfloat16)


def place(doc_rows, retrieved, key_new, value_new, positions):
    served, tokens = positions.shape
    width = key_new.shape[1]
    heads = width // HD
    count = served * retrieved
    placed = jax.ShapeDtypeStruct((count, 2, doc_rows, HD), jnp.bfloat16)
    return pl.pallas_call(
        functools.partial(place_kernel, retrieved, doc_rows),
        grid=(served,),
        in_specs=[
            pl.BlockSpec((tokens, width), lambda r: (r, 0)),
            pl.BlockSpec((tokens, width), lambda r: (r, 0)),
            pl.BlockSpec((1, 1, tokens), lambda r: (r, 0, 0)),
        ],
        out_specs=[pl.BlockSpec((retrieved, doc_rows, HD), lambda r: (r, 0, 0))]
        + [pl.BlockSpec((retrieved, 2, doc_rows, HD), lambda r: (r, 0, 0, 0))] * heads,
        out_shape=[jax.ShapeDtypeStruct((count, doc_rows, HD), jnp.bfloat16)] + [placed] * heads,
        compiler_params=pltpu.CompilerParams(vmem_limit_bytes=VMEM_GRANT),
        cost_estimate=pl.CostEstimate(
            flops=2 * count * doc_rows * 256 * (2 * heads + 1) * HD,
            bytes_accessed=2 * count * doc_rows * (2 * heads + 1) * HD,
            transcendentals=0,
        ),
    )(key_new, value_new, positions[:, None, :])


def attention_kernel(retrieved, doc_rows, tokens, slots, lens, *refs):
    docs = refs[:retrieved]
    q_ref, keep, placed, pos_col, o_ref = refs[retrieved : retrieved + 5]
    keys, values, scores = refs[retrieved + 5 :]
    group = H // KVH
    picks = tokens // retrieved
    span = PAIR * picks
    wide = PAIR * doc_rows
    per_doc = doc_rows // LANES
    factor = HD ** (-0.5) * LOG2E
    first_doc = pl.program_id(0) * retrieved
    block = pl.program_id(1)
    half = group // 2
    first_heads = tuple(range(half))
    second_heads = tuple(range(half, group))

    @pl.when(block == 0)
    def blend():
        for j in range(retrieved):
            rows = slice(j * doc_rows, (j + 1) * doc_rows)
            keys[:, rows] = (docs[j][0, 0] * keep[j] + placed[j, 0]).T
            values[rows, :] = docs[j][0, 1] * keep[j] + placed[j, 1]

    def rows_of(g):
        return slice(g * span, (g + 1) * span)

    def some(heads):
        return slice(heads[0] * span, (heads[-1] + 1) * span)

    def columns_of(n):
        return slice(n * LANES, (n + 1) * LANES)

    def run(last):
        top, total, acc = {}, {}, {}

        def score(p, heads):
            query = jnp.concatenate([q_ref[:, columns_of(g)] for g in heads], axis=0)
            raw = jnp.dot(
                query, keys[:, p * wide : (p + 1) * wide], preferred_element_type=jnp.float32
            )
            for n in range(wide // LANES):
                doc = p * PAIR + n // per_doc
                limit = lens[first_doc + doc] - 1
                if p == last:
                    limit = jnp.minimum(pos_col[...] - doc * doc_rows, limit)
                rows = span if p == last else 1
                lane = lax.broadcasted_iota(jnp.int32, (rows, LANES), 1)
                mask = lane + (n % per_doc) * LANES <= limit
                for at, g in enumerate(heads):
                    part = jnp.where(mask, raw[at * span : (at + 1) * span, columns_of(n)], MASKED)
                    scores[p, rows_of(g), columns_of(n)] = part
                    top[g] = jnp.maximum(top[g], part) if g in top else part

        def settle_top(heads):
            for g in heads:
                top[g] = jnp.max(top[g], axis=1, keepdims=True) * factor

        def exponent(p, heads):
            for g in heads:
                for n in range(wide // LANES):
                    expo = jnp.exp2(scores[p, rows_of(g), columns_of(n)] * factor - top[g])
                    scores[p, rows_of(g), columns_of(n)] = expo
                    total[g] = total[g] + expo if g in total else expo

        def settle_total(heads):
            for g in heads:
                total[g] = 1.0 / jnp.sum(total[g], axis=1, keepdims=True)

        def combine(p, heads):
            weights = jnp.concatenate(
                [
                    (scores[p, rows_of(g), :] * total[g]).astype(jnp.bfloat16)
                    for g in heads
                ],
                axis=0,
            )
            term = jnp.dot(
                weights, values[p * wide : (p + 1) * wide, :], preferred_element_type=jnp.float32
            )
            acc[heads] = acc[heads] + term if heads in acc else term

        def finish(heads):
            for at, g in enumerate(heads):
                o_ref[:, columns_of(g)] = acc[heads][at * span : (at + 1) * span].astype(o_ref.dtype)

        pairs = range(last + 1)
        for p in pairs:
            score(p, first_heads)
        settle_top(first_heads)
        for p in pairs:
            score(p, second_heads)
            exponent(p, first_heads)
        settle_top(second_heads)
        settle_total(first_heads)
        for p in pairs:
            exponent(p, second_heads)
            combine(p, first_heads)
        finish(first_heads)
        settle_total(second_heads)
        for p in pairs:
            combine(p, second_heads)
        finish(second_heads)

    for last in range(retrieved // PAIR):
        pl.when(block == last)(functools.partial(run, last))


def attention(head, cache, slots, lens, query, keep, placed, positions):
    served, tokens = positions.shape
    retrieved = slots.shape[0] // served
    doc_rows = cache.shape[2]
    group = H // KVH
    span = tokens // retrieved * PAIR
    blocks = retrieved // PAIR
    rows = group * span
    doc_specs = [
        pl.BlockSpec(
            (1, 2, doc_rows, HD),
            lambda r, b, slots, lens, j=j: (slots[r * retrieved + j], 0, 0, 0),
        )
        for j in range(retrieved)
    ]
    pairs = served * tokens * group * retrieved * doc_rows * 5 // 8
    return pl.pallas_call(
        functools.partial(attention_kernel, retrieved, doc_rows, tokens),
        grid_spec=pltpu.PrefetchScalarGridSpec(
            num_scalar_prefetch=2,
            grid=(served, blocks),
            in_specs=doc_specs
            + [
                pl.BlockSpec((span, group * HD), lambda r, b, *_: (r * blocks + b, head)),
                pl.BlockSpec((retrieved, doc_rows, HD), lambda r, b, *_: (r, 0, 0)),
                pl.BlockSpec((retrieved, 2, doc_rows, HD), lambda r, b, *_: (r, 0, 0, 0)),
                pl.BlockSpec((span, 1), lambda r, b, *_: (r * blocks + b, 0)),
            ],
            out_specs=pl.BlockSpec((span, group * HD), lambda r, b, *_: (r * blocks + b, 0)),
            scratch_shapes=[
                pltpu.VMEM((HD, retrieved * doc_rows), jnp.bfloat16),
                pltpu.VMEM((retrieved * doc_rows, HD), jnp.bfloat16),
                pltpu.VMEM((blocks, rows, PAIR * doc_rows), jnp.float32),
            ],
        ),
        out_shape=jax.ShapeDtypeStruct((served * tokens, group * HD), jnp.bfloat16),
        compiler_params=pltpu.CompilerParams(vmem_limit_bytes=VMEM_GRANT),
        cost_estimate=pl.CostEstimate(
            flops=8 * pairs * HD,
            bytes_accessed=2 * served * retrieved * doc_rows * 5 * HD,
            transcendentals=pairs,
        ),
    )(
        slots,
        lens,
        *([cache] * retrieved),
        query,
        keep,
        placed,
        positions.reshape(served * tokens, 1),
    )


def chained_product(attn, w_out, head, kv_local):
    size = lax.axis_size("tp")
    at = lax.axis_index("tp")
    depth = attn.shape[1]

    def rows_for(step):
        shard = lax.rem(at - step + size, size)
        return lax.dynamic_slice_in_dim(w_out, (shard * kv_local + head) * depth, depth, 0)

    def product(block, step):
        return jnp.dot(block, rows_for(step), preferred_element_type=jnp.float32)

    right, left = [attn], [attn]
    for step in range(1, size):
        up = [(n, n + 1) for n in range(step - 1, size - 1)]
        right.append(lax.ppermute(right[-1], "tp", up))
        left.append(lax.ppermute(left[-1], "tp", [(size - 1 - a, size - 1 - b) for a, b in up]))
    out = product(attn, 0)
    for step in sorted(range(1, size), key=lambda n: max(n, size - n)):
        out = out + product(right[step] + left[size - step], step)
    return out


def body(
    sel_hidden,
    norm_gain,
    w_query,
    w_key,
    w_value,
    w_out,
    doc_cache,
    home,
    doc_ids,
    doc_len,
    positions,
):
    groups = lax.axis_size("grp")
    me = lax.axis_index("grp")
    stored = doc_cache.shape[0]
    doc_rows = doc_cache.shape[2]
    width = doc_cache.shape[3]
    kv_local = width // HD
    group = H // KVH
    served = sel_hidden.shape[0]
    tokens = sel_hidden.shape[1]
    retrieved = doc_ids.shape[1]
    per_group = served * retrieved
    location = home[doc_ids].reshape(groups, per_group)
    owner = location // stored
    slot_index = location % stored
    slots = jnp.arange(per_group, dtype=jnp.int32)
    earlier = (owner[:, :, None] == owner[:, None, :]) & (
        slots[None, None, :] < slots[None, :, None]
    )
    rank = jnp.sum(earlier.astype(jnp.int32), axis=2)
    match = (owner == me)[:, :, None] & (
        rank[:, :, None] == jnp.arange(CAP, dtype=jnp.int32)[None, None, :]
    )
    chosen = jnp.sum(jnp.where(match, slot_index[:, :, None], 0), axis=1)
    own_slots = owner[me] * CAP + rank[me]
    lengths = doc_len[doc_ids.reshape(groups, per_group)[me]]

    incoming = []
    for head in range(kv_local):
        outgoing = pick(head, chosen.reshape(groups * CAP), doc_cache).reshape(
            groups, CAP, 2, doc_rows, HD
        )
        if incoming:
            outgoing, incoming[-1] = lax.optimization_barrier((outgoing, incoming[-1]))
        incoming.append(
            lax.all_to_all(outgoing, "grp", split_axis=0, concat_axis=0, tiled=True)
        )

    xf = sel_hidden.astype(jnp.float32)
    normed = (xf * lax.rsqrt(jnp.mean(xf * xf, axis=-1, keepdims=True) + 1e-05) * norm_gain).astype(
        jnp.bfloat16
    )
    normed_rows = normed.reshape(served * tokens, normed.shape[2])
    query = jnp.dot(normed_rows, w_query, preferred_element_type=jnp.float32).astype(jnp.bfloat16)
    key_new = jnp.dot(normed_rows, w_key, preferred_element_type=jnp.float32).astype(jnp.bfloat16)
    value_new = jnp.dot(normed_rows, w_value, preferred_element_type=jnp.float32).astype(
        jnp.bfloat16
    )

    keep, *placed = place(doc_rows, retrieved, key_new, value_new, positions)
    w_heads = w_out.reshape(-1, kv_local, group * HD, w_out.shape[1])
    mixed = 0.0
    for head in range(kv_local):
        cache = incoming[head].reshape((groups * CAP, 2, doc_rows, HD))
        attn = attention(
            head, cache, own_slots, lengths, query, keep, placed[head], positions
        )
        if head < kv_local - 1:
            gathered = lax.all_gather(attn, "tp", axis=1, tiled=True)
            part = w_heads[:, head].reshape(-1, w_out.shape[1])
            mixed = mixed + jnp.dot(gathered, part, preferred_element_type=jnp.float32)
        else:
            mixed = mixed + chained_product(attn, w_out, head, kv_local)
    return mixed.astype(jnp.bfloat16).reshape(served, tokens, w_out.shape[1])


def solution(mesh):
    return jax.shard_map(
        body,
        mesh=mesh,
        in_specs=(
            P("grp", None, None),
            P(),
            P(None, "tp"),
            P(None, "tp"),
            P(None, "tp"),
            P(None, "tp"),
            P("grp", None, None, "tp"),
            P(),
            P(),
            P(),
            P("grp", None),
        ),
        out_specs=P("grp", None, "tp"),
        check_vma=False,
    )
```

time: 242 us -> 231 us (0.955)
  local copies, waits for them, and re-layouts: 30.9 us -> 10.7 us
  starting transfers between devices: 10.3 us -> 21.1 us
    all_gather x4 -> x1, waiting for transfers between devices: 46.3 us -> 0.01 us  [body(): gathered = lax.all_gather(attn, 'tp', axis=1, tiled=True)]
    ppermute x0 -> x6, waiting for transfers between devices: none -> 38.9 us  [the longest x3 38.9 us: chained_product(): lax.ppermute(left[-1], 'tp', [(size - 1 - a, size - 1 - b) for a, b in up])]
    pallas_call x4 -> x2, Pallas kernels: 66.4 us -> 42.7 us  [attention(): pl.pallas_call(functools.partial(attention_kernel, retrieved, doc_rows, t...]
    unnamed x45 -> x27, local copies, waits for them, and re-layouts: 21.6 us -> 1.01 us
    pallas_call x2, Pallas kernels: 3.6 us -> 21.8 us  [pick(): pl.pallas_call(pick_kernel, grid_spec=pltpu.PrefetchScalarGridSpec(num_sc...]
    ppermute x0 -> x6, starting transfers between devices: none -> 11 us  [the longest x3 7.12 us: chained_product(): right.append(lax.ppermute(right[-1], 'tp', up))]
    all_to_all x2, waiting for transfers between devices: 25.4 us -> 31.6 us  [body(): lax.all_to_all(outgoing, 'grp', split_axis=0, concat_axis=0, tiled=True)]
    pallas_call x1, Pallas kernels: 3.75 us -> 6.92 us  [place(): pl.pallas_call(functools.partial(place_kernel, retrieved, doc_rows), grid...]
  transfers between devices with their start and end apart: 6 -> 9, of which waited for: 4 -> 5; matrix products, arithmetic and copies ran while one was open for 17% -> 19% of each run, Pallas kernels for 30% -> 26%
where the time goes in v2:
time: 231 us; the launch traced here: 229 us
  Pallas kernels  71.4 us (31%)
  waiting for transfers between devices  70.6 us (31%)
  matrix products  31.9 us (14%)
  starting transfers between devices  21.1 us (9%)
  between operations  13.7 us (6%)
  local copies, waits for them, and re-layouts  10.7 us (5%)
  other arithmetic  9.9 us (4%)
    pallas_call x2, Pallas kernels, attention(): pl.pallas_call(functools.partial(attention_kernel, retrieved, doc_rows, t...  42.7 us
    ppermute x3, waiting for transfers between devices, chained_product(): lax.ppermute(left[-1], 'tp', [(size - 1 - a, size - 1 - b) for a, b in up])  38.9 us
    all_to_all x2, waiting for transfers between devices, body(): lax.all_to_all(outgoing, 'grp', split_axis=0, concat_axis=0, tiled=True)  31.6 us
    pallas_call x2, Pallas kernels, pick(): pl.pallas_call(pick_kernel, grid_spec=pltpu.PrefetchScalarGridSpec(num_sc...  21.8 us
    dot_general x4, matrix products, product(): return jnp.dot(block, rows_for(step), preferred_element_type=jnp.float32)  11.6 us
    dot_general x1, matrix products, body(): jnp.dot(normed_rows, w_query, preferred_element_type=jnp.float32)  10.4 us
    all_to_all x2, starting transfers between devices, body(): lax.all_to_all(outgoing, 'grp', split_axis=0, concat_axis=0, tiled=True)  9.87 us
    ppermute x3, starting transfers between devices, chained_product(): right.append(lax.ppermute(right[-1], 'tp', up))  7.12 us
  transfers between devices with their start and end apart: 9, of which 5 were waited for; matrix products, arithmetic and copies ran while one was open for 19% of the time, Pallas kernels for 26%

profile of v2, /device:TPU:0, one launch (start us, length us, event | category | flops | bytes accessed | tf_op | source)
XLA Modules:
  0.0 229.2 jit_solution(10594849067451285951)
XLA Ops:
  6.5 0.0 copy-start
  6.6 0.8 compare_select_fusion
  7.4 0.1 copy.18
  7.5 0.1 reshape.191
  7.6 0.0 copy-done.2
  7.6 1.2 gather_fusion
  8.8 0.1 reshape.178
  8.9 0.3 convert_reduce_fusion
  9.2 0.2 select_reduce_fusion
  9.4 0.1 copy.20
  9.4 0.6 reshape.180.chosen
  10.0 10.8 %shard_map.110 = bf16[16,2,512,128]{3,2,1,0:T(8,128)(2,1)} custom-call(s32[16]{0:T(128)} %reshape.180.chosen, bf16[16,2,512,256]{3,2,1,0:T(8,128)(2,1)} %cache.3), custom_call_target="tpu_custom_call" | custom-call | bytes 8388608 | tf_op jit(solution)/shard_map/pallas_call | solution.py:28
  20.9 5.3 %all-to-all-start = ((bf16[8,2,2,512,128]{4,3,2,1,0:T(8,128)(2,1)}), bf16[8,2,2,512,128]{4,3,2,1,0:T(8,128)(2,1)}, u32[]{:S(2)}, u32[]{:S(2)}) async-start(bf16[8,2,2,512,128]{4,3,2,1,0:T(8,128)(2,1)} %bitcast.28), calls=%async_computation | async-start | bytes 8388608 | tf_op jit(solution)/shard_map/all_to_all | solution.py:319
  26.2 0.0 copy-done.10
  26.2 0.1 copy.19
  26.3 11.0 %shard_map.109 = bf16[16,2,512,128]{3,2,1,0:T(8,128)(2,1)} custom-call(s32[16]{0:T(128)} %reshape.180.chosen, bf16[16,2,512,256]{3,2,1,0:T(8,128)(2,1)} %cache.3), custom_call_target="tpu_custom_call" | custom-call | bytes 8388608 | tf_op jit(solution)/shard_map/pallas_call | solution.py:28
  37.2 0.0 copy-done.11
  37.2 0.6 broadcast_in_dim.19.pos_lane
  37.8 1.0 reshape.208.refs_11_
  38.8 0.1 reshape.179
  38.9 0.0 copy-done.3
  38.9 1.3 gather_fusion.1
  40.1 0.6 fusion.27.slots
  40.7 3.6 %fusion = f32[2,320]{1,0:T(2,128)S(1)} fusion(bf16[2,320,4096]{2,1,0:T(8,128)(2,1)} %param.11), kind=kLoop, calls=%fused_computation.4 | loop fusion | flops 7863680 | bytes 5245440 | tf_op jit(solution)/shard_map/reduce_sum | solution.py:323
  44.3 0.0 copy-done.9
  44.3 4.4 %fusion.2 = bf16[2,320,4096]{2,1,0:T(8,128)(2,1)S(1)} fusion(bf16[2,320,4096]{2,1,0:T(8,128)(2,1)} %param.11, f32[4096]{0:T(1024)S(1)} %copy-done.9, f32[2,320]{1,0:T(2,128)S(1)} %add_rsqrt_fusion), kind=kLoop, calls=%fused_computation.6 | loop fusion | flops 10485760 | bytes 10504704 | tf_op jit(solution)/shard_map/convert_element_type | solution.py:323
  48.7 0.0 copy-start.5
  48.7 0.0 copy-done
  48.7 0.0 copy-start.12
  48.8 2.3 convolution_convert_fusion.2.new_k
  51.0 0.3 copy-done.5
  51.3 0.6 copy-done.12
  51.9 2.3 convolution_convert_fusion.1.new_v
  54.2 6.9 %shard_map.111 = (bf16[16,512,128]{2,1,0:T(8,128)(2,1)}, bf16[16,2,512,128]{3,2,1,0:T(8,128)(2,1)}, bf16[16,2,512,128]{3,2,1,0:T(8,128)(2,1)}) custom-call(bf16[640,256]{1,0:T(8,128)(2,1)} %convolution_convert_fusion.2.new_k, bf16[640,256]{1,0:T(8,128)(2,1)} %convolution_convert_fusion.1.new_v, s32[2,1,320]{2,1,0:T(1,128)} %broadcast_in_dim.19.pos_lane), custom_call_target="tpu_custom_call" | custom-call | flops 2684354560 | bytes 10485760 | tf_op jit(solution)/shard_map/pallas_call | solution.py:69
  61.1 14.3 %all-to-all-done = bf16[8,2,2,512,128]{4,3,2,1,0:T(8,128)(2,1)} async-done(((bf16[8,2,2,512,128]{4,3,2,1,0:T(8,128)(2,1)}), bf16[8,2,2,512,128]{4,3,2,1,0:T(8,128)(2,1)}, u32[]{:S(2)}, u32[]{:S(2)}) %all-to-all-start) | async-done | bytes 4194336 | tf_op jit(solution)/shard_map/all_to_all | solution.py:319
  75.4 4.6 %all-to-all-start.1 = ((bf16[8,2,2,512,128]{4,3,2,1,0:T(8,128)(2,1)}), bf16[8,2,2,512,128]{4,3,2,1,0:T(8,128)(2,1)}, u32[]{:S(2)}, u32[]{:S(2)}) async-start(bf16[8,2,2,512,128]{4,3,2,1,0:T(8,128)(2,1)} %bitcast.27), calls=%async_computation.1 | async-start | bytes 8388608 | tf_op jit(solution)/shard_map/all_to_all | solution.py:319
  80.0 0.2 all-gather.2.cloned.1.call-start
  80.2 10.4 %convolution_convert_fusion.refs_8_ = bf16[640,1024]{1,0:T(8,128)(2,1)} fusion(bf16[640,4096]{1,0:T(8,128)(2,1)} %bitcast.32, bf16[4096,1024]{1,0:T(8,128)(2,1)} %param.13), kind=kOutput, calls=%fused_computation.8 | convolution fusion | flops 5369364480 | bytes 14942208 | tf_op jit(solution)/shard_map/dot_general | solution.py:327
  90.6 21.2 %shard_map.112 = bf16[640,512]{1,0:T(8,128)(2,1)} custom-call(s32[16]{0:T(128)} %fusion.27.slots, s32[16]{0:T(128)} %gather_fusion.1, bf16[16,2,512,128]{3,2,1,0:T(8,128)(2,1)} %bitcast.5.refs_0_.refs_1_.refs_2_.refs_3_.refs_4_.refs_5_.refs_6_.refs_7_, bf16[16,2,512,128]{3,2,1,0:T(8,128)(2,1)} %bitcast.5.refs_0_.refs_1_.refs_2_.refs_3_.refs_4_.refs_5_.refs_6_.refs_7_, ...), custom_call_target="tpu_custom_call" | custom-call | flops 6710886400 | bytes 10485760 | tf_op jit(solution)/shard_map/pallas_call | solution.py:212
  111.8 0.0 all-gather.2.cloned.1.call-update
  111.8 17.3 %all-to-all-done.1 = bf16[8,2,2,512,128]{4,3,2,1,0:T(8,128)(2,1)} async-done(((bf16[8,2,2,512,128]{4,3,2,1,0:T(8,128)(2,1)}), bf16[8,2,2,512,128]{4,3,2,1,0:T(8,128)(2,1)}, u32[]{:S(2)}, u32[]{:S(2)}) %all-to-all-start.1) | async-done | bytes 4194336 | tf_op jit(solution)/shard_map/all_to_all | solution.py:319
  129.1 21.5 %shard_map.113 = bf16[640,512]{1,0:T(8,128)(2,1)} custom-call(s32[16]{0:T(128)} %fusion.27.slots, s32[16]{0:T(128)} %gather_fusion.1, bf16[16,2,512,128]{3,2,1,0:T(8,128)(2,1)} %bitcast.9.refs_0_.refs_1_.refs_2_.refs_3_.refs_4_.refs_5_.refs_6_.refs_7_, bf16[16,2,512,128]{3,2,1,0:T(8,128)(2,1)} %bitcast.9.refs_0_.refs_1_.refs_2_.refs_3_.refs_4_.refs_5_.refs_6_.refs_7_, ...), custom_call_target="tpu_custom_call" | custom-call | flops 6710886400 | bytes 10485760 | tf_op jit(solution)/shard_map/pallas_call | solution.py:212
  150.6 1.3 collective-permute-start.2
  151.9 4.9 %collective-permute-start = (bf16[640,512]{1,0:T(8,128)(2,1)}, bf16[640,512]{1,0:T(8,128)(2,1)S(1)}, u32[]{:S(2)}, u32[]{:S(2)}) collective-permute-start(bf16[640,512]{1,0:T(8,128)(2,1)} %shard_map.113), channel_id=1, source_target_pairs={{0,1},{1,2},{2,3},{4,5},{5,6},{6,7},{8,9},{9,10},{10,11},{12,13},{... | collective-permute-start | bytes 1966088 | tf_op jit(solution)/shard_map/ppermute | solution.py:264
  156.8 24.0 %collective-permute-done.2 = bf16[640,512]{1,0:T(8,128)(2,1)S(1)} collective-permute-done((bf16[640,512]{1,0:T(8,128)(2,1)}, bf16[640,512]{1,0:T(8,128)(2,1)S(1)}, u32[]{:S(2)}, u32[]{:S(2)}) %collective-permute-start.2) | collective-permute-done | bytes 655392 | tf_op jit(solution)/shard_map/ppermute | solution.py:265
  180.8 1.3 collective-permute-start.3
  182.1 0.0 collective-permute-done
  182.1 0.7 collective-permute-start.1
  182.8 0.0 copy-start.6
  182.8 4.6 %slice.8 = bf16[4,1,512,1024]{3,2,1,0:T(8,128)(2,1)} slice(bf16[4,2,512,1024]{3,2,1,0:T(8,128)(2,1)} %bitcast.29), slice={[0:4], [0:1], [0:512], [0:1024]} | slice | bytes 8388608 | tf_op jit(solution)/shard_map/slice | solution.py:343
  187.5 0.0 copy-done.7
  187.5 0.0 copy-done.6
  187.5 3.6 %fusion.11 = f32[640,1024]{1,0:T(8,128)} fusion(bf16[640,512]{1,0:T(8,128)(2,1)S(1)} %copy-done.6, bf16[4096,1024]{1,0:T(8,128)(2,1)} %param.16, s32[]{:T(128)S(6)} %select_n.67), kind=kOutput, calls=%fused_computation.17 | convolution fusion | flops 671088640 | bytes 4325380 | tf_op jit(solution)/shard_map/dot_general | solution.py:259
  191.1 8.0 %collective-permute-done.3 = bf16[640,512]{1,0:T(8,128)(2,1)S(1)} collective-permute-done((bf16[640,512]{1,0:T(8,128)(2,1)S(1)}, bf16[640,512]{1,0:T(8,128)(2,1)S(1)}, u32[]{:S(2)}, u32[]{:S(2)}) %collective-permute-start.3) | collective-permute-done | bytes 655392 | tf_op jit(solution)/shard_map/ppermute | solution.py:265
  199.1 1.3 collective-permute-start.4
  200.3 0.0 collective-permute-done.1
  200.4 1.5 collective-permute-start.5
  201.9 5.4 %fusion.28 = f32[640,1024]{1,0:T(8,128)S(1)} fusion(bf16[640,2048]{1,0:T(8,128)(2,1)} %all-gather.2.cloned.1.call-done, bf16[2048,1024]{1,0:T(8,128)(2,1)} %bitcast.33), kind=kOutput, calls=%fused_computation.53 | convolution fusion | flops 2684354560 | bytes 9437184 | tf_op jit(solution)/shard_map/dot_general | solution.py:344
  207.3 2.1 fusion.9
  209.4 0.0 copy-start.8
  209.4 7.0 %collective-permute-done.4 = bf16[640,512]{1,0:T(8,128)(2,1)} collective-permute-done((bf16[640,512]{1,0:T(8,128)(2,1)S(1)}, bf16[640,512]{1,0:T(8,128)(2,1)}, u32[]{:S(2)}, u32[]{:S(2)}) %collective-permute-start.4) | collective-permute-done | bytes 655392 | tf_op jit(solution)/shard_map/ppermute | solution.py:265
  216.4 2.4 %fusion.7 = f32[640,1024]{1,0:T(8,128)S(1)} fusion(bf16[4096,1024]{1,0:T(8,128)(2,1)} %param.16, s32[]{:T(128)S(6)} %select_n.69, bf16[640,512]{1,0:T(8,128)(2,1)S(1)} %collective-permute-done, bf16[640,512]{1,0:T(8,128)(2,1)} %collective-permute-done.4), kind=kOutput, calls=%fused_computation.13 | convolution fusion | flops 671416320 | bytes 4980740 | tf_op jit(solution)/shard_map/dot_general | solution.py:259
  218.8 0.0 collective-permute-done.5
  218.8 3.5 %add_convert_fusion = bf16[640,1024]{1,0:T(8,128)(2,1)} fusion(f32[640,1024]{1,0:T(8,128)S(1)} %fusion.28, f32[640,1024]{1,0:T(8,128)S(1)} %fusion.7, f32[640,1024]{1,0:T(8,128)S(1)} %copy-done.4, f32[640,1024]{1,0:T(8,128)S(1)} %fusion.9, bf16[4096,1024]{1,0:T(8,128)(2,1)} %param.16, s32[]{:T(128)S(6)} %select_n.70, ...), kind=kOutput, calls=%fused_computation.7 | convolution fusion | flops 674693120 | bytes 14155780 | tf_op jit(solution)/shard_map/dot_general | solution.py:259
  (19 shorter events, 0.1 us)
Async XLA Ops:
  6.5 42.2 %copy-start = (bf16[4096,256]{1,0:T(8,128)(2,1)S(1)}, bf16[4096,256]{1,0:T(8,128)(2,1)}, u32[]{:S(2)}) copy-start(bf16[4096,256]{1,0:T(8,128)(2,1)} %param.14) | copy-start | bytes 6291460
  6.5 1.0 copy-start.2
  20.9 5.3 %copy-start.10 = (s32[16,8]{0,1:T(8,128)S(1)}, s32[16,8]{0,1:T(8,128)}, u32[]{:S(2)}) copy-start(s32[16,8]{0,1:T(8,128)} %param.19) | copy-start | bytes 1540
  20.9 54.5 %all-to-all-start = ((bf16[8,2,2,512,128]{4,3,2,1,0:T(8,128)(2,1)}), bf16[8,2,2,512,128]{4,3,2,1,0:T(8,128)(2,1)}, u32[]{:S(2)}, u32[]{:S(2)}) async-start(bf16[8,2,2,512,128]{4,3,2,1,0:T(8,128)(2,1)} %bitcast.28), calls=%async_computation | async-start | bytes 8388608 | tf_op jit(solution)/shard_map/all_to_all | solution.py:319
  26.3 11.0 %copy-start.11 = (s32[2,320]{1,0:T(2,128)S(1)}, s32[2,320]{1,0:T(2,128)}, u32[]{:S(2)}) copy-start(s32[2,320]{1,0:T(2,128)} %param.21) | copy-start | bytes 7684
  26.3 12.6 %copy-start.3 = (s32[128]{0:T(128)S(1)}, s32[128]{0:T(128)}, u32[]{:S(2)}) copy-start(s32[128]{0:T(128)} %param.20) | copy-start | bytes 1540
  37.2 7.1 %copy-start.9 = (f32[4096]{0:T(1024)S(1)}, f32[4096]{0:T(1024)}, u32[]{:S(2)}) copy-start(f32[4096]{0:T(1024)} %param.12) | copy-start | bytes 49156
  48.7 2.6 %copy-start.5 = (bf16[2,320,4096]{2,1,0:T(8,128)(2,1)}, bf16[2,320,4096]{2,1,0:T(8,128)(2,1)S(1)}, u32[]{:S(2)}) copy-start(bf16[2,320,4096]{2,1,0:T(8,128)(2,1)S(1)} %fusion.2) | copy-start | bytes 15728644
  48.7 3.2 %copy-start.12 = (bf16[4096,256]{1,0:T(8,128)(2,1)S(1)}, bf16[4096,256]{1,0:T(8,128)(2,1)}, u32[]{:S(2)}) copy-start(bf16[4096,256]{1,0:T(8,128)(2,1)} %param.15) | copy-start | bytes 6291460
  75.4 53.7 %all-to-all-start.1 = ((bf16[8,2,2,512,128]{4,3,2,1,0:T(8,128)(2,1)}), bf16[8,2,2,512,128]{4,3,2,1,0:T(8,128)(2,1)}, u32[]{:S(2)}, u32[]{:S(2)}) async-start(bf16[8,2,2,512,128]{4,3,2,1,0:T(8,128)(2,1)} %bitcast.27), calls=%async_computation.1 | async-start | bytes 8388608 | tf_op jit(solution)/shard_map/all_to_all | solution.py:319
  80.0 121.9 %all-gather.2.cloned.1.call-start = ((), (), s32[]{:S(2)}) async-start(), calls=%async_computation.2 | async-start | bytes 3276800 | tf_op jit(solution)/shard_map/all_gather | solution.py:342
  150.6 30.2 %collective-permute-start.2 = (bf16[640,512]{1,0:T(8,128)(2,1)}, bf16[640,512]{1,0:T(8,128)(2,1)S(1)}, u32[]{:S(2)}, u32[]{:S(2)}) collective-permute-start(bf16[640,512]{1,0:T(8,128)(2,1)} %shard_map.113), channel_id=1, source_target_pairs={{3,2},{2,1},{1,0},{7,6},{6,5},{5,4},{11,10},{10,9},{9,8},{15,14},{... | collective-permute-start | bytes 1966088 | tf_op jit(solution)/shard_map/ppermute | solution.py:265
  151.9 30.2 %collective-permute-start = (bf16[640,512]{1,0:T(8,128)(2,1)}, bf16[640,512]{1,0:T(8,128)(2,1)S(1)}, u32[]{:S(2)}, u32[]{:S(2)}) collective-permute-start(bf16[640,512]{1,0:T(8,128)(2,1)} %shard_map.113), channel_id=1, source_target_pairs={{0,1},{1,2},{2,3},{4,5},{5,6},{6,7},{8,9},{9,10},{10,11},{12,13},{... | collective-permute-start | bytes 1966088 | tf_op jit(solution)/shard_map/ppermute | solution.py:264
  180.8 6.7 %copy-start.7 = (bf16[640,512]{1,0:T(8,128)(2,1)}, bf16[640,512]{1,0:T(8,128)(2,1)S(1)}, u32[]{:S(2)}) copy-start(bf16[640,512]{1,0:T(8,128)(2,1)S(1)} %collective-permute-done.2) | copy-start | bytes 1966084
  180.8 18.3 %collective-permute-start.3 = (bf16[640,512]{1,0:T(8,128)(2,1)S(1)}, bf16[640,512]{1,0:T(8,128)(2,1)S(1)}, u32[]{:S(2)}, u32[]{:S(2)}) collective-permute-start(bf16[640,512]{1,0:T(8,128)(2,1)S(1)} %collective-permute-done.2), channel_id=1, source_target_pairs={{2,1},{1,0},{6,5},{5,4},{10,9},{9,8},{14,13},{13,12},{18,17},{17,1... | collective-permute-start | bytes 1966088 | tf_op jit(solution)/shard_map/ppermute | solution.py:265
  182.1 18.3 %collective-permute-start.1 = (bf16[640,512]{1,0:T(8,128)(2,1)S(1)}, bf16[640,512]{1,0:T(8,128)(2,1)S(1)}, u32[]{:S(2)}, u32[]{:S(2)}) collective-permute-start(bf16[640,512]{1,0:T(8,128)(2,1)S(1)} %collective-permute-done), channel_id=1, source_target_pairs={{1,2},{2,3},{5,6},{6,7},{9,10},{10,11},{13,14},{14,15},{17,18},{18... | collective-permute-start | bytes 1966088 | tf_op jit(solution)/shard_map/ppermute | solution.py:264
  182.8 4.7 %copy-start.6 = (bf16[640,512]{1,0:T(8,128)(2,1)S(1)}, bf16[640,512]{1,0:T(8,128)(2,1)}, u32[]{:S(2)}) copy-start(bf16[640,512]{1,0:T(8,128)(2,1)} %shard_map.113) | copy-start | bytes 1966084
  199.1 17.3 %collective-permute-start.4 = (bf16[640,512]{1,0:T(8,128)(2,1)S(1)}, bf16[640,512]{1,0:T(8,128)(2,1)}, u32[]{:S(2)}, u32[]{:S(2)}) collective-permute-start(bf16[640,512]{1,0:T(8,128)(2,1)S(1)} %collective-permute-done.3), channel_id=1, source_target_pairs={{1,0},{5,4},{9,8},{13,12},{17,16},{21,20},{25,24},{29,28}} | collective-permute-start | bytes 1966088 | tf_op jit(solution)/shard_map/ppermute | solution.py:265
  200.4 18.4 %collective-permute-start.5 = (bf16[640,512]{1,0:T(8,128)(2,1)S(1)}, bf16[640,512]{1,0:T(8,128)(2,1)}, u32[]{:S(2)}, u32[]{:S(2)}) collective-permute-start(bf16[640,512]{1,0:T(8,128)(2,1)S(1)} %collective-permute-done.1), channel_id=1, source_target_pairs={{2,3},{6,7},{10,11},{14,15},{18,19},{22,23},{26,27},{30,31}} | collective-permute-start | bytes 1966088 | tf_op jit(solution)/shard_map/ppermute | solution.py:264
  209.4 9.4 %copy-start.4 = (f32[640,1024]{1,0:T(8,128)S(1)}, f32[640,1024]{1,0:T(8,128)}, u32[]{:S(2)}) copy-start(f32[640,1024]{1,0:T(8,128)} %fusion.11) | copy-start | bytes 7864324
  209.4 9.4 %copy-start.8 = (bf16[640,512]{1,0:T(8,128)(2,1)S(1)}, bf16[640,512]{1,0:T(8,128)(2,1)}, u32[]{:S(2)}) copy-start(bf16[640,512]{1,0:T(8,128)(2,1)} %copy-done.7) | copy-start | bytes 1966084
  216.4 5.9 %copy-start.1 = (bf16[4096,256]{1,0:T(8,128)(2,1)S(1)}, bf16[4096,256]{1,0:T(8,128)(2,1)}, u32[]{:S(2)}) copy-start(bf16[4096,256]{1,0:T(8,128)(2,1)} %param.14) | copy-start | bytes 6291460
Sparse Core Ops, SparseCore 0:
  111.9 62.7 all-gather.1
